TPU v7x, 512 devices: a whole 4x8x8 slice. The times are simulated.
512 devices in a mesh: section: 16 (over x, y_lo), peer: 32 (over y_hi, z, core).
Axes of the slice: x: 4, y: 8 (y_hi: 2, y_lo: 4; y = y_hi * 4 + y_lo), z: 8, core: 2. Of those that a mesh axis runs over, the one named last changes fastest.
Arguments:
- hidden_in: bfloat16 [32, 128, 4096], P('peer', None, 'section'), may hold values from -6 to 6
- cotangent: bfloat16 [32, 128, 4096], P('peer', None, 'section'), may hold values from -24 to 24
- norm_gain: float32 [16, 4096], P('section'), may hold values from 0.1 to 1.9
- adapter_down: bfloat16 [16, 32, 4096, 32], P('section', 'peer'), may hold values from -6 to 6
- adapter_up: bfloat16 [16, 32, 32, 4096], P('section', 'peer'), may hold values from -6 to 6
- moment_down: bfloat16 [16, 32, 4096, 32], P('section', 'peer'), may hold values from -6 to 6
- moment_up: bfloat16 [16, 32, 32, 4096], P('section', 'peer'), may hold values from -6 to 6
- square_down: bfloat16 [16, 32, 4096, 32], P('section', 'peer'), may hold values from 0.0009994507 to 0.019897461
- square_up: bfloat16 [16, 32, 32, 4096], P('section', 'peer'), may hold values from 0.0009994507 to 0.019897461
- round_bits: int32 [4], replicated, may hold values from 0 to 4, as said below
Outputs:
- peer_down: bfloat16 [16, 32, 4096, 32], P('section', 'peer')
- peer_up: bfloat16 [16, 32, 32, 4096], P('section', 'peer')
- peer_moment_down: bfloat16 [16, 32, 4096, 32], P('section', 'peer')
- peer_moment_up: bfloat16 [16, 32, 32, 4096], P('section', 'peer')
- peer_square_down: bfloat16 [16, 32, 4096, 32], P('section', 'peer')
- peer_square_up: bfloat16 [16, 32, 32, 4096], P('section', 'peer')
Inputs may be any that keep to these rules, and one draw needn't show every extreme that they name: `round_bits`: bit 0 and the highest bit are each named by some round; other rounds may name any bit, repeats allowed.
All inputs are finite; a program needn't handle non-finite values.
Results may differ from a plain program's by a relative error of at most 0.03.
Values may be sent and summed in bfloat16 or wider, within the bound.
A program may use at most 64 MiB of HBM per device.

v0:
```python
from functools import partial

import jax
import jax.numpy as jnp
from jax import lax
from jax.sharding import PartitionSpec as P

ROUNDS = 4
ADAM_STEP = 100


def shortened(shard):
    return jax.tree.map(lambda a: a.astype(jnp.bfloat16) if a.dtype == jnp.float32 else a, shard)


def from_partner(shard, axis, bit):
    return lax.ppermute(shard, axis, [(i, i ^ 1 << bit) for i in range(lax.axis_size(axis))])


def shifted(value, axis, steps):
    count = lax.axis_size(axis)
    first, last = (max(0, -steps), min(count, count - steps))
    return lax.ppermute(value, axis, [(source, source + steps) for source in range(first, last)])


def normalize(hidden, gain):
    values = hidden.astype(jnp.float32)
    scale = lax.rsqrt(jnp.mean(values * values, axis=-1, keepdims=True) + 1e-05)
    normed = (values * scale * gain).astype(jnp.bfloat16)
    return (values, scale, normed)


def layer_forward(hidden, gain, down, upper):
    values, scale, normed = normalize(hidden, gain)
    width = hidden.shape[-1]
    rank = down.shape[-1]
    latent = (jnp.dot(normed, down, preferred_element_type=jnp.float32) * width ** (-0.5)).astype(
        jnp.bfloat16
    )
    delta = jnp.dot(latent, upper, preferred_element_type=jnp.float32) * rank ** (-0.5)
    return (values + delta).astype(jnp.bfloat16)


def layer_backward(hidden, grad_out, gain, down, upper):
    values, scale, normed = normalize(hidden, gain)
    width = hidden.shape[-1]
    rank = down.shape[-1]
    latent = (jnp.dot(normed, down, preferred_element_type=jnp.float32) * width ** (-0.5)).astype(
        jnp.bfloat16
    )
    grad_up = lax.dot_general(
        latent, grad_out, (((0,), (0,)), ((), ())), preferred_element_type=jnp.float32
    ) * rank ** (-0.5)
    inner = (
        lax.dot_general(
            grad_out, upper, (((1,), (1,)), ((), ())), preferred_element_type=jnp.float32
        )
        * rank ** (-0.5)
    ).astype(jnp.bfloat16)
    grad_down = lax.dot_general(
        normed, inner, (((0,), (0,)), ((), ())), preferred_element_type=jnp.float32
    ) * width ** (-0.5)
    grad_normed = lax.dot_general(
        inner, down, (((1,), (1,)), ((), ())), preferred_element_type=jnp.float32
    ) * width ** (-0.5)
    weighted = grad_normed * gain
    project = jnp.mean(values * weighted, axis=-1, keepdims=True)
    grad_in = scale * weighted - values * scale * scale * scale * project
    return ((grad_out.astype(jnp.float32) + grad_in).astype(jnp.bfloat16), grad_down, grad_up)


def adam_step(param, first, second, grad):
    first_new = 0.9 * first.astype(jnp.float32) + 0.1 * grad
    second_new = 0.999 * second.astype(jnp.float32) + 0.001 * grad * grad
    corr_one = 1.0 - 0.9**ADAM_STEP
    corr_two = 1.0 - 0.999**ADAM_STEP
    update = 0.05 * (first_new / corr_one) / (jnp.sqrt(second_new / corr_two) + 1e-08)
    return (
        (param.astype(jnp.float32) - update).astype(jnp.bfloat16),
        first_new.astype(jnp.bfloat16),
        second_new.astype(jnp.bfloat16),
    )


def pair_mean(state, bit_number):
    partner = jax.tree.map(
        lambda part, own: part.astype(own.dtype),
        from_partner(shortened(state), "peer", bit_number),
        state,
    )
    return ((state.astype(jnp.float32) + partner.astype(jnp.float32)) * 0.5).astype(jnp.bfloat16)


def on_device(
    hidden_in,
    cotangent,
    norm_gain,
    adapter_down,
    adapter_up,
    moment_down,
    moment_up,
    square_down,
    square_up,
    round_bits,
):
    whole_hidden, whole_cotangent = (
        lax.all_gather(hidden_in, "section", axis=2, tiled=True),
        lax.all_gather(cotangent, "section", axis=2, tiled=True),
    )
    section_count = lax.axis_size("section")
    section_index = lax.axis_index("section")
    gain = norm_gain[0]
    down = adapter_down[0, 0]
    upper = adapter_up[0, 0]
    token_count = whole_hidden.shape[1]
    width = whole_hidden.shape[2]
    block_count = section_count // 2
    block_rows = token_count // block_count
    first_blocks = whole_hidden[0].reshape(block_count, block_rows, width)
    last_blocks = whole_cotangent[0].reshape(block_count, block_rows, width)
    turns = block_count + section_count - 1

    def forward_turn(turn, carry):
        previous, saved = carry
        incoming = shifted(previous, "section", 1)
        block = turn - section_index
        valid = (block >= 0) & (block < block_count)
        clipped = jnp.clip(block, 0, block_count - 1)
        fresh = lax.dynamic_index_in_dim(first_blocks, clipped, 0, keepdims=False)
        hidden = jnp.where(section_index == 0, fresh, incoming)
        updated = lax.dynamic_update_index_in_dim(saved, hidden, clipped, 0)
        saved = jnp.where(valid, updated, saved)
        return (layer_forward(hidden, gain, down, upper), saved)

    start = (
        jnp.zeros((block_rows, width), jnp.bfloat16),
        jnp.zeros((block_count, block_rows, width), jnp.bfloat16),
    )
    unused, saved = lax.fori_loop(0, turns, forward_turn, start)

    def backward_turn(turn, carry):
        previous, total_down, total_up = carry
        incoming = shifted(previous, "section", -1)
        block = turn - (section_count - 1 - section_index)
        valid = (block >= 0) & (block < block_count)
        clipped = jnp.clip(block, 0, block_count - 1)
        fresh = lax.dynamic_index_in_dim(last_blocks, clipped, 0, keepdims=False)
        grad_out = jnp.where(section_index == section_count - 1, fresh, incoming)
        hidden = lax.dynamic_index_in_dim(saved, clipped, 0, keepdims=False)
        grad_in, grad_down, grad_up = layer_backward(hidden, grad_out, gain, down, upper)
        total_down = total_down + jnp.where(valid, grad_down, 0.0)
        total_up = total_up + jnp.where(valid, grad_up, 0.0)
        return (grad_in, total_down, total_up)

    begin = (
        jnp.zeros((block_rows, width), jnp.bfloat16),
        jnp.zeros(down.shape, jnp.float32),
        jnp.zeros(upper.shape, jnp.float32),
    )
    unused_grad, total_down, total_up = lax.fori_loop(0, turns, backward_turn, begin)
    new_down, mom_down, sq_down = adam_step(down, moment_down[0, 0], square_down[0, 0], total_down)
    new_up, mom_up, sq_up = adam_step(upper, moment_up[0, 0], square_up[0, 0], total_up)
    state = jnp.stack(
        [
            new_down.reshape(-1),
            new_up.reshape(-1),
            mom_down.reshape(-1),
            mom_up.reshape(-1),
            sq_down.reshape(-1),
            sq_up.reshape(-1),
        ]
    )
    peer_bits = lax.axis_size("peer").bit_length() - 1
    branches = [partial(pair_mean, bit_number=number) for number in range(peer_bits)]
    for round_number in range(ROUNDS):
        state = lax.switch(round_bits[round_number], branches, state)
    down_shape = (1, 1) + down.shape
    up_shape = (1, 1) + upper.shape
    return (
        state[0].reshape(down_shape),
        state[1].reshape(up_shape),
        state[2].reshape(down_shape),
        state[3].reshape(up_shape),
        state[4].reshape(down_shape),
        state[5].reshape(up_shape),
    )


def solution(mesh):
    in_specs = (
        P("peer", None, "section"),
        P("peer", None, "section"),
        P("section", None),
        P("section", "peer", None, None),
        P("section", "peer", None, None),
        P("section", "peer", None, None),
        P("section", "peer", None, None),
        P("section", "peer", None, None),
        P("section", "peer", None, None),
        P(),
    )
    out_specs = (
        P("section", "peer", None, None),
        P("section", "peer", None, None),
        P("section", "peer", None, None),
        P("section", "peer", None, None),
        P("section", "peer", None, None),
        P("section", "peer", None, None),
    )
    return jax.shard_map(
        on_device, mesh=mesh, in_specs=in_specs, out_specs=out_specs, check_vma=False
    )
```

profile of v0, /device:TPU:2, one launch (start us, length us, event | category | flops | bytes accessed | tf_op | source)
XLA Modules:
  0.0 1046.7 jit_solution(12251651110443606107)
XLA Ops:
  14.1 73.3 %all-gather.5.cloned.1.call-done = bf16[1,128,4096]{2,1,0:T(8,128)(2,1)} async-done(((bf16[1,128,256]{2,1,0:T(8,128)(2,1)}), bf16[1,128,4096]{2,1,0:T(8,128)(2,1)}) %all-gather.5.cloned.1.call-update) | async-done | bytes 1048592 | tf_op jit(solution)/shard_map/all_gather | solution.py:107
  87.5 76.0 %all-gather.3.cloned.1.call-done = bf16[1,128,4096]{2,1,0:T(8,128)(2,1)} async-done(((bf16[1,128,256]{2,1,0:T(8,128)(2,1)}), bf16[1,128,4096]{2,1,0:T(8,128)(2,1)}) %all-gather.3.cloned.1.call-update) | async-done | bytes 1048592 | tf_op jit(solution)/shard_map/all_gather | solution.py:108
  164.5 279.8 %while.37 = (s32[]{:T(128)}, bf16[16,4096]{1,0:T(8,128)(2,1)S(1)}, bf16[8,16,4096]{2,1,0:T(8,128)(2,1)}, pred[]{:T(512)}, s32[]{:T(128)}, /*index=5*/bf16[8,16,4...) while((s32[]{:T(128)}, bf16[16,4096]{1,0:T(8,128)(2,1)S(1)}, ...), condition=%wide.region_2.3_spmd.clone, body=%wide.region_0.2_spmd.clone.sunk | while | flops 9307161 | bytes 2376685 | solution.py:139
  167.1 8.4 collective-permute-done.20
  179.8 8.1 collective-permute-done.20
  192.2 7.6 collective-permute-done.20
  204.1 7.6 collective-permute-done.20
  216.0 7.6 collective-permute-done.20
  227.9 7.6 collective-permute-done.20
  239.8 7.6 collective-permute-done.20
  251.7 7.6 collective-permute-done.20
  263.6 7.6 collective-permute-done.20
  275.5 8.1 collective-permute-done.20
  287.9 8.8 collective-permute-done.20
  301.0 8.0 collective-permute-done.20
  313.3 7.6 collective-permute-done.20
  325.2 7.6 collective-permute-done.20
  337.1 7.6 collective-permute-done.20
  360.9 7.6 collective-permute-done.20
  372.8 7.6 collective-permute-done.20
  396.7 8.3 collective-permute-done.20
  421.1 8.9 collective-permute-done.20
  434.3 7.7 collective-permute-done.20
  444.4 363.5 %while.38 = (s32[]{:T(128)}, bf16[16,4096]{1,0:T(8,128)(2,1)S(1)}, f32[4096,32]{0,1:T(8,128)S(1)}, f32[32,4096]{1,0:T(8,128)S(1)}, pred[]{:T(512)}, /*index=5*/s...) while((s32[]{:T(128)}, bf16[16,4096]{1,0:T(8,128)(2,1)S(1)}, ...), condition=%wide.region_6.7_spmd.clone, body=%wide.region_3.6_spmd.clone.sunk | while | flops 23730200 | bytes 5722001 | solution.py:160
  818.8 9.1 stack.18
  827.9 8.2 conditional.5
  836.1 52.0 %conditional.6 = (bf16[6,131072]{1,0:T(8,128)(2,1)S(1)}) conditional(s32[]{:T(128)} %bitcast.2, bf16[6,131072]{1,0:T(8,128)(2,1)} %get-tuple-element.1074, bf16[6,131072]{1,0:T(8,128)(2,1)} %get-tuple-element.1074, bf16[6,131072]{1,0:T(8,128)(2,1)} %get-tuple-element.1074, ...), branch_computations={%region_12.13_spmd, %region_13.14_spmd, %region_14.15_spmd, %regio... | conditional | flops 3932160 | bytes 11010096 | solution.py:176
  838.9 47.1 %collective-permute-done.6 = bf16[6,131072]{1,0:T(8,128)(2,1)S(1)} collective-permute-done((bf16[6,131072]{1,0:T(8,128)(2,1)}, bf16[6,131072]{1,0:T(8,128)(2,1)S(1)}, u32[]{:S(2)}, u32[]{:S(2)}) %collective-permute-start.6) | collective-permute-done | bytes 1572896 | tf_op jit(solution)/shard_map/cond/branch_1_fun/ppermute | solution.py:17
  888.2 8.0 conditional.7
  896.1 142.4 %conditional.8 = (bf16[6,131072]{1,0:T(8,128)(2,1)}, bf16[1,131072]{1,0:T(2,128)(2,1)}, bf16[1,131072]{1,0:T(2,128)(2,1)}, bf16[1,131072]{1,0:T(2,128)(2,1)}, bf...) conditional(s32[]{:T(128)} %bitcast, ...), branch_computations={%region_22.23_spmd, %region_23.24_spmd, %region_24.25_spmd, %regio... | conditional | flops 3932160 | bytes 26738860
  920.3 94.4 %collective-permute-done.19 = bf16[6,131072]{1,0:T(8,128)(2,1)S(1)} collective-permute-done((bf16[6,131072]{1,0:T(8,128)(2,1)}, bf16[6,131072]{1,0:T(8,128)(2,1)S(1)}, u32[]{:S(2)}, u32[]{:S(2)}) %collective-permute-start.19) | collective-permute-done | bytes 1572896 | tf_op jit(solution)/shard_map/cond/branch_4_fun/ppermute | solution.py:17
  1016.9 16.6 %fusion.75 = (bf16[131072]{0:T(1024)(128)(2,1)S(1)}, bf16[1,131072]{1,0:T(2,128)(2,1)S(1)}, bf16[131072]{0:T(1024)(128)(2,1)S(1)}, bf16[1,131072]{1,0:T(2,128)(2...) fusion(bf16[6,131072]{1,0:T(8,128)(2,1)S(1)} %add_multiply_fusion.4), kind=kLoop, calls=%fused_computation.114 | loop fusion | bytes 4718592 | tf_op jit(solution)/shard_map/slice | solution.py:185
  (449 shorter events, 532.0 us)
Async XLA Ops:
  7.2 80.3 %all-gather.5.cloned.1.call-start = ((), (), s32[]{:S(2)}) async-start(), calls=%async_computation.1 | async-start | bytes 1114112 | tf_op jit(solution)/shard_map/all_gather | solution.py:107
  7.9 155.5 %all-gather.3.cloned.1.call-start = ((), (), s32[]{:S(2)}) async-start(), calls=%async_computation | async-start | bytes 1114112 | tf_op jit(solution)/shard_map/all_gather | solution.py:108
  164.6 10.9 %collective-permute-start.20 = (bf16[16,4096]{1,0:T(8,128)(2,1)S(1)}, bf16[16,4096]{1,0:T(8,128)(2,1)S(1)}, u32[]{:S(2)}, u32[]{:S(2)}) collective-permute-start(bf16[16,4096]{1,0:T(8,128)(2,1)S(1)} %broadcast_select_fusion.4), channel_id=1, source_target_pairs={{0,32},{32,64},{64,96},{96,128},{128,160},{160,192},{192,224},{224... | collective-permute-start | bytes 393224 | tf_op jit(solution)/shard_map/while/body/eval_jaxpr/ppermute | solution.py:23
  177.8 10.0 collective-permute-start.20
  273.6 10.0 collective-permute-start.20
  286.0 10.7 %collective-permute-start.20 = (bf16[16,4096]{1,0:T(8,128)(2,1)S(1)}, bf16[16,4096]{1,0:T(8,128)(2,1)S(1)}, u32[]{:S(2)}, u32[]{:S(2)}) collective-permute-start(bf16[16,4096]{1,0:T(8,128)(2,1)S(1)} %broadcast_select_fusion.4), channel_id=1, source_target_pairs={{0,32},{32,64},{64,96},{96,128},{128,160},{160,192},{192,224},{224... | collective-permute-start | bytes 393224 | tf_op jit(solution)/shard_map/while/body/eval_jaxpr/ppermute | solution.py:23
  299.1 9.9 collective-permute-start.20
  394.7 10.2 collective-permute-start.20
  419.2 10.8 %collective-permute-start.20 = (bf16[16,4096]{1,0:T(8,128)(2,1)S(1)}, bf16[16,4096]{1,0:T(8,128)(2,1)S(1)}, u32[]{:S(2)}, u32[]{:S(2)}) collective-permute-start(bf16[16,4096]{1,0:T(8,128)(2,1)S(1)} %broadcast_select_fusion.4), channel_id=1, source_target_pairs={{0,32},{32,64},{64,96},{96,128},{128,160},{160,192},{192,224},{224... | collective-permute-start | bytes 393224 | tf_op jit(solution)/shard_map/while/body/eval_jaxpr/ppermute | solution.py:23
  432.4 9.7 collective-permute-start.20
  471.3 9.6 collective-permute-start.21
  487.3 9.6 collective-permute-start.21
  503.2 9.6 collective-permute-start.21
  519.2 9.6 collective-permute-start.21
  535.1 9.6 collective-permute-start.21
  551.1 10.5 %collective-permute-start.21 = (bf16[16,4096]{1,0:T(8,128)(2,1)S(1)}, bf16[16,4096]{1,0:T(8,128)(2,1)S(1)}, u32[]{:S(2)}, u32[]{:S(2)}) collective-permute-start(bf16[16,4096]{1,0:T(8,128)(2,1)S(1)} %broadcast_select_fusion.5), channel_id=1, source_target_pairs={{32,0},{64,32},{96,64},{128,96},{160,128},{192,160},{224,192},{256... | collective-permute-start | bytes 393224 | tf_op jit(solution)/shard_map/while/body/eval_jaxpr/ppermute | solution.py:23
  568.0 10.2 collective-permute-start.21
  584.6 9.6 collective-permute-start.21
  616.5 9.6 collective-permute-start.21
  632.5 9.6 collective-permute-start.21
  648.4 9.6 collective-permute-start.21
  664.4 9.6 collective-permute-start.21
  680.3 9.6 collective-permute-start.21
  696.3 9.6 collective-permute-start.21
  712.2 9.6 collective-permute-start.21
  728.2 9.6 collective-permute-start.21
  744.1 9.6 collective-permute-start.21
  760.1 9.6 collective-permute-start.21
  776.0 9.6 collective-permute-start.21
  792.0 9.6 collective-permute-start.21
  836.2 49.8 %collective-permute-start.6 = (bf16[6,131072]{1,0:T(8,128)(2,1)}, bf16[6,131072]{1,0:T(8,128)(2,1)S(1)}, u32[]{:S(2)}, u32[]{:S(2)}) collective-permute-start(bf16[6,131072]{1,0:T(8,128)(2,1)} %param.10), channel_id=1, source_target_pairs={{0,2},{1,3},{2,0},{3,1},{4,6},{5,7},{6,4},{7,5},{8,10},{9,11},{10,... | collective-permute-start | bytes 4718600 | tf_op jit(solution)/shard_map/cond/branch_1_fun/ppermute | solution.py:17
  915.6 99.0 %collective-permute-start.19 = (bf16[6,131072]{1,0:T(8,128)(2,1)}, bf16[6,131072]{1,0:T(8,128)(2,1)S(1)}, u32[]{:S(2)}, u32[]{:S(2)}) collective-permute-start(bf16[6,131072]{1,0:T(8,128)(2,1)} %param.23), channel_id=1, source_target_pairs={{0,16},{1,17},{2,18},{3,19},{4,20},{5,21},{6,22},{7,23},{8,24},{9,... | collective-permute-start | bytes 4718600 | tf_op jit(solution)/shard_map/cond/branch_4_fun/ppermute | solution.py:17
  (27 other events, 876.4 us)
Sparse Core Ops, SparseCore 0:
  10.0 77.3 all-gather.4
  89.5 73.9 all-gather.2
where the time goes:
time: 1060 us; the launch traced here: 1050 us
  waiting for transfers between devices  542 us (51%)
  starting transfers between devices  211 us (20%)
  matrix products  111 us (10%)
  other arithmetic  99.8 us (9%)
  local copies, waits for them, and re-layouts  43.1 us (4%)
  loops' own time  23.2 us (2%)
  between operations  17.3 us (2%)
    ppermute x46, waiting for transfers between devices, shifted(): lax.ppermute(value, axis, [(source, source + steps) for source in range(f...  241 us
    ppermute x46, starting transfers between devices, shifted(): lax.ppermute(value, axis, [(source, source + steps) for source in range(f...  200 us
    ppermute x4, waiting for transfers between devices, from_partner(): lax.ppermute(shard, axis, [(i, i ^ 1 << bit) for i in range(lax.axis_size...  150 us
    all_gather x1, waiting for transfers between devices, on_device(): lax.all_gather(cotangent, 'section', axis=2, tiled=True)  76 us
    all_gather x1, waiting for transfers between devices, on_device(): lax.all_gather(hidden_in, 'section', axis=2, tiled=True)  73.3 us
    select_n x23, other arithmetic, forward_turn(): saved = jnp.where(valid, updated, saved)  38.4 us
    dot_general x23, matrix products, layer_backward(): lax.dot_general(latent, grad_out, (((0,), (0,)), ((), ())), preferred_ele...  34.8 us
    dot_general x23, matrix products, layer_backward(): lax.dot_general(inner, down, (((1,), (1,)), ((), ())), preferred_element_...  32.6 us
  transfers between devices with their start and end apart: 52, of which 52 were waited for; matrix products, arithmetic and copies ran while one was open for 0% of the time, Pallas kernels for 0%

commit v1 on v0

v1 whole, which is shorter than its diff:
```python
import jax
import jax.numpy as jnp
from jax import lax
from jax.experimental import pallas as pl
from jax.experimental.pallas import tpu as pltpu
from jax.sharding import PartitionSpec as P

ADAM_STEP = 100
MESH = pl.DeviceIdType.MESH
F32, BF16 = jnp.float32, jnp.bfloat16
SECTIONS, NX, NY = 16, 4, 4
RANK, WIDTH, TOKENS = 32, 4096, 128
SLICE = WIDTH // SECTIONS
ALL = SECTIONS * RANK
XW = ALL + 3 * TOKENS
VMEM = pl.BlockSpec(memory_space=pltpu.VMEM)
LIMIT = 48 << 20

NN = (((1,), (0,)), ((), ()))
NT = (((1,), (1,)), ((), ()))


def dot(a, b, dims=NN):
    return lax.dot_general(a, b, dims, preferred_element_type=F32)


def block_masks():
    row = lax.broadcasted_iota(jnp.int32, (ALL, ALL), 0) // RANK
    col = lax.broadcasted_iota(jnp.int32, (ALL, ALL), 1) // RANK
    return row > col, row < col


def remote(src, dst, send, recv, section, peer):
    return pltpu.make_async_remote_copy(
        src_ref=src, dst_ref=dst, send_sem=send, recv_sem=recv, device_id=(section, peer), device_id_type=MESH
    )


def products_kernel(
    h_ref, q_ref, g_ref, a_ref, b_ref, x_ref, n_ref, af_ref, bf_ref,
    scaled, part, rx, px, ry, npart, nrx, npx, nry, sa, ra, sb, rb, sx, rxs, sn, rn, sy, rys, sm, rm, sg, rg, sh, rh,
):
    me, peer = lax.axis_index("section"), lax.axis_index("peer")
    mx, my = me // NY, me % NY

    barrier = pltpu.get_barrier_semaphore()
    for j in range(1, SECTIONS):
        pl.semaphore_signal(barrier, inc=1, device_id=((me + j) % SECTIONS, peer), device_id_type=MESH)
    scaled[...] = (a_ref[...].astype(F32) * (g_ref[...] * WIDTH**-0.5)).astype(BF16)
    pl.semaphore_wait(barrier, SECTIONS - 1)

    mine = pl.ds(pl.multiple_of(me * RANK, RANK), RANK)
    copies = []
    for j in range(1, SECTIONS):
        to = (me + j) % SECTIONS
        cols = pl.ds(pl.multiple_of(to * SLICE, SLICE), SLICE)
        copies.append(remote(scaled.at[:, cols], af_ref.at[mine], sa.at[j], ra.at[j], to, peer))
        copies.append(remote(b_ref.at[:, cols], bf_ref.at[mine], sb.at[j], rb.at[j], to, peer))
    for copy in copies:
        copy.start()
    cols = pl.ds(pl.multiple_of(me * SLICE, SLICE), SLICE)
    af_ref[mine, :] = scaled[:, cols]
    bf_ref[mine, :] = b_ref[:, cols]
    h = h_ref[...]
    square = h.astype(F32) * h.astype(F32)
    high = square.astype(BF16)
    low = (square - high.astype(F32)).astype(BF16)
    ones = jnp.ones((8, SLICE), BF16)
    npart[...] = dot(ones, high, NT) + dot(ones, low, NT)
    for copy in copies:
        copy.wait()

    af, bf = af_ref[...], bf_ref[...]
    rs = RANK**-0.5
    lower, _ = block_masks()
    part[:, 0:ALL] = jnp.where(lower, dot(af, bf, NT) * rs, dot(bf, bf, NT) * (1.0 / RANK)).astype(BF16)
    part[:, ALL : ALL + TOKENS] = dot(af, h, NT).astype(BF16)
    part[:, ALL + TOKENS : ALL + 2 * TOKENS] = (dot(bf, h, NT) * rs).astype(BF16)
    part[:, ALL + 2 * TOKENS : XW] = (dot(bf, q_ref[...], NT) * rs).astype(BF16)

    group = NY * RANK

    def group_rows(x):
        return pl.ds(pl.multiple_of(x * group, group), group)

    copies = []
    for j in range(1, NX):
        x = (mx + j) % NX
        copies.append(remote(part.at[group_rows(x)], rx.at[j - 1], sx.at[j], rxs.at[j], x * NY + my, peer))
        copies.append(remote(npart, nrx.at[j - 1], sn.at[j], rn.at[j], x * NY + my, peer))
    for copy in copies:
        copy.start()
    for copy in copies:
        copy.wait()
    total = part[group_rows(mx), :].astype(F32)
    for j in range(NX - 1):
        total += rx[j].astype(F32)
    px[...] = total.astype(BF16)
    npx[...] = npart[...] + nrx[0] + nrx[1] + nrx[2]

    def rank_rows(y):
        return pl.ds(pl.multiple_of(y * RANK, RANK), RANK)

    copies = []
    for j in range(1, NY):
        y = (my + j) % NY
        copies.append(remote(px.at[rank_rows(y)], ry.at[j - 1], sy.at[j], rys.at[j], mx * NY + y, peer))
        copies.append(remote(npx, nry.at[j - 1], sm.at[j], rm.at[j], mx * NY + y, peer))
    for copy in copies:
        copy.start()
    for copy in copies:
        copy.wait()
    total = px[rank_rows(my), :].astype(F32)
    for j in range(NY - 1):
        total += ry[j].astype(F32)
    x_ref[mine, :] = total.astype(BF16)
    n_ref[...] = npx[...] + nry[0] + nry[1] + nry[2]

    copies = []
    for j in range(1, NY):
        to = mx * NY + (my + j) % NY
        copies.append(remote(x_ref.at[mine], x_ref.at[mine], sg.at[j], rg.at[j], to, peer))
    for copy in copies:
        copy.start()
    for copy in copies:
        copy.wait()
    copies = []
    for j in range(1, NX):
        to = ((mx + j) % NX) * NY + my
        copies.append(remote(x_ref.at[group_rows(mx)], x_ref.at[group_rows(mx)], sh.at[j], rh.at[j], to, peer))
    for copy in copies:
        copy.start()
    for copy in copies:
        copy.wait()


def products(h, q, gain, a, b):
    dma = pltpu.SemaphoreType.DMA
    group = NY * RANK
    return pl.pallas_call(
        products_kernel,
        out_shape=(
            jax.ShapeDtypeStruct((ALL, XW), BF16),
            jax.ShapeDtypeStruct((8, TOKENS), F32),
            jax.ShapeDtypeStruct((ALL, SLICE), BF16),
            jax.ShapeDtypeStruct((ALL, SLICE), BF16),
        ),
        in_specs=[VMEM] * 5,
        out_specs=(VMEM,) * 4,
        scratch_shapes=[
            pltpu.VMEM((RANK, WIDTH), BF16),
            pltpu.VMEM((ALL, XW), BF16),
            pltpu.VMEM((NX - 1, group, XW), BF16),
            pltpu.VMEM((group, XW), BF16),
            pltpu.VMEM((NY - 1, RANK, XW), BF16),
            pltpu.VMEM((8, TOKENS), F32),
            pltpu.VMEM((NX - 1, 8, TOKENS), F32),
            pltpu.VMEM((8, TOKENS), F32),
            pltpu.VMEM((NY - 1, 8, TOKENS), F32),
        ]
        + [dma((SECTIONS,))] * 4
        + [dma((4,))] * 12,
        compiler_params=pltpu.CompilerParams(collective_id=0, has_side_effects=True, vmem_limit_bytes=LIMIT),
        name="products",
    )(h, q, gain, a, b)


def chain_kernel(x_ref, n_ref, af_ref, bf_ref, h_ref, q_ref, gd_ref, gu_ref, xt, lat, scaled_inner, cl, wp, rms):
    rs = RANK**-0.5
    xt[...] = x_ref[:, 0:ALL].astype(F32).T.astype(BF16)

    def rows(s):
        return slice(RANK * s, RANK * s + RANK)

    norm = n_ref[0:1, :]
    for s in range(SECTIONS):
        u = x_ref[rows(s), ALL : ALL + TOKENS].astype(F32)
        w = x_ref[rows(s), ALL + TOKENS : ALL + 2 * TOKENS].astype(F32)
        if s > 0:
            before = lat[0 : RANK * s, :]
            u += dot(x_ref[rows(s), 0 : RANK * s], before)
            w += dot(xt[rows(s), 0 : RANK * s], before)
        r = lax.rsqrt(jnp.maximum(norm, 0.0) * (1.0 / WIDTH) + 1e-5)
        latent = (u * r).astype(BF16)
        lat[rows(s), :] = latent
        after = w + dot(xt[rows(s), rows(s)], latent)
        norm += jnp.sum(latent.astype(F32) * (w + after), axis=0, keepdims=True)
        wp[rows(s), :] = after
        rms[s : s + 1, :] = r

    carry = jnp.zeros((1, TOKENS), F32)
    for s in reversed(range(SECTIONS)):
        inner = x_ref[rows(s), ALL + 2 * TOKENS : XW].astype(F32) - carry * wp[rows(s), :]
        if s < SECTIONS - 1:
            later = RANK * (s + 1)
            inner += dot(xt[rows(s), later:ALL], scaled_inner[later:ALL, :])
            inner -= dot(x_ref[rows(s), later:ALL], cl[later:ALL, :])
        r = rms[s : s + 1, :]
        latent = lat[rows(s), :].astype(F32)
        scaled_inner[rows(s), :] = (r * inner).astype(BF16)
        cl[rows(s), :] = (carry * latent).astype(BF16)
        carry += r * r * (jnp.sum(latent * inner, axis=0, keepdims=True) * (1.0 / WIDTH))

    lower, upper = block_masks()
    af, bf, h = af_ref[...], bf_ref[...], h_ref[...]
    ls, ri, cls = lat[...], scaled_inner[...], cl[...]
    down = dot(ri, h) + dot(jnp.where(lower, dot(ri, ls, NT), 0.0).astype(BF16), bf) * rs
    gd_ref[...] = (down * WIDTH**-0.5).astype(BF16)
    mixed = jnp.where(upper, dot(ls, cls, NT), dot(cls, ls, NT)).astype(BF16)
    up = dot(ls, q_ref[...]) - dot(cls, h) - dot(mixed, bf) * rs
    up += dot(jnp.where(upper, dot(ls, ri, NT), 0.0).astype(BF16), af)
    gu_ref[...] = (up * rs).astype(BF16)


def chain(x, n, af, bf, h, q):
    return pl.pallas_call(
        chain_kernel,
        out_shape=(jax.ShapeDtypeStruct((ALL, SLICE), BF16),) * 2,
        in_specs=[VMEM] * 6,
        out_specs=(VMEM,) * 2,
        scratch_shapes=[
            pltpu.VMEM((ALL, ALL), BF16),
            pltpu.VMEM((ALL, TOKENS), BF16),
            pltpu.VMEM((ALL, TOKENS), BF16),
            pltpu.VMEM((ALL, TOKENS), BF16),
            pltpu.VMEM((ALL, TOKENS), F32),
            pltpu.VMEM((SECTIONS, TOKENS), F32),
        ],
        compiler_params=pltpu.CompilerParams(vmem_limit_bytes=LIMIT),
        name="chain",
    )(x, n, af, bf, h, q)


def adam(param, first, second, grad):
    first_new = 0.9 * first.astype(F32) + 0.1 * grad
    second_new = 0.999 * second.astype(F32) + 0.001 * grad * grad
    corr_one = 1.0 - 0.9**ADAM_STEP
    corr_two = 1.0 - 0.999**ADAM_STEP
    update = 0.05 * (first_new / corr_one) / (jnp.sqrt(second_new / corr_two) + 1e-08)
    return param.astype(F32) - update, first_new, second_new


def make_update(bits, number):
    near = tuple(b for b in bits if b != 4)
    steps = [(b, "split") for b in near] + [(4, "swap")] + [(b, "join") for b in reversed(near)]
    widths = {b: WIDTH >> (i + 1) for i, b in enumerate(near)}
    widths[4] = WIDTH >> len(near)

    def kernel(gd_ref, gu_ref, g_ref, a_ref, b_ref, ma_ref, mb_ref, va_ref, vb_ref, out, work, gdf, gup, sd, rd, su, ru, ss, sr, *landing):
        me, peer = lax.axis_index("section"), lax.axis_index("peer")
        land = dict(zip(near + (4,), landing))
        barrier = pltpu.get_barrier_semaphore()
        for j in range(1, SECTIONS):
            pl.semaphore_signal(barrier, inc=1, device_id=((me + j) % SECTIONS, peer), device_id_type=MESH)
        for b in bits:
            pl.semaphore_signal(barrier, inc=1, device_id=(me, peer ^ (1 << b)), device_id_type=MESH)
        pl.semaphore_wait(barrier, SECTIONS - 1 + len(bits))

        mine = pl.ds(pl.multiple_of(me * SLICE, SLICE), SLICE)
        copies = []
        for j in range(1, SECTIONS):
            to = (me + j) % SECTIONS
            rows = pl.ds(pl.multiple_of(to * RANK, RANK), RANK)
            copies.append(remote(gd_ref.at[rows], gdf.at[:, mine], sd.at[j], rd.at[j], to, peer))
            copies.append(remote(gu_ref.at[rows], gup.at[:, mine], su.at[j], ru.at[j], to, peer))
        for copy in copies:
            copy.start()
        rows = pl.ds(pl.multiple_of(me * RANK, RANK), RANK)
        gdf[:, mine] = gd_ref[rows, :]
        gup[:, mine] = gu_ref[rows, :]
        for copy in copies:
            copy.wait()

        def step(i, _):
            cols = pl.ds(pl.multiple_of(i * 512, 512), 512)
            grad = gdf[:, cols].astype(F32) * g_ref[:, cols]
            new = adam(a_ref[:, cols], ma_ref[:, cols], va_ref[:, cols], grad)
            other = adam(b_ref[:, cols], mb_ref[:, cols], vb_ref[:, cols], gup[:, cols].astype(F32))
            for k, value in enumerate((new[0], other[0], new[1], other[1], new[2], other[2])):
                work[RANK * k : RANK * k + RANK, cols] = value.astype(BF16)
            return 0

        lax.fori_loop(0, WIDTH // 512, step, 0)

        start = 0
        for number_of, (b, kind) in enumerate(steps):
            bit = (peer // (1 << b)) % 2
            to = peer + (1 - 2 * bit) * (1 << b)
            width = widths[b]
            if kind == "split":
                keep = pl.ds(pl.multiple_of(start + bit * width, width), width)
                give = pl.ds(pl.multiple_of(start + (1 - bit) * width, width), width)
                copy = remote(work.at[:, give], land[b], ss.at[number_of], sr.at[number_of], me, to)
                start = start + bit * width
            elif kind == "swap":
                keep = pl.ds(pl.multiple_of(start, width), width)
                copy = remote(work.at[:, keep], land[b], ss.at[number_of], sr.at[number_of], me, to)
            else:
                keep = pl.ds(pl.multiple_of(start, width), width)
                copy = remote(out.at[:, keep], out.at[:, keep], ss.at[number_of], sr.at[number_of], me, to)
                start = start - bit * width
            copy.start()
            copy.wait()
            if kind != "join":
                mean = ((work[:, keep].astype(F32) + land[b][...].astype(F32)) * 0.5).astype(BF16)
                if kind == "split":
                    work[:, keep] = mean
                else:
                    out[:, keep] = mean

    dma = pltpu.SemaphoreType.DMA

    def update(gd, gu, gain, *state):
        return pl.pallas_call(
            kernel,
            out_shape=jax.ShapeDtypeStruct((6 * RANK, WIDTH), BF16),
            in_specs=[VMEM] * 9,
            out_specs=VMEM,
            scratch_shapes=[pltpu.VMEM((6 * RANK, WIDTH), BF16)]
            + [pltpu.VMEM((RANK, WIDTH), BF16)] * 2
            + [dma((SECTIONS,))] * 4
            + [dma((len(steps),))] * 2
            + [pltpu.VMEM((6 * RANK, widths[b]), BF16) for b in near + (4,)],
            compiler_params=pltpu.CompilerParams(
                collective_id=1 + number, has_side_effects=True, vmem_limit_bytes=LIMIT
            ),
            name=f"update_{number}",
        )(gd, gu, gain, *state)

    return update


CASES = [(0, 4), (0, 1, 4), (0, 2, 4), (0, 3, 4), (0, 1, 2, 4), (0, 1, 3, 4), (0, 2, 3, 4)]
CASE_OF_MASK = [0, 1, 2, 4, 3, 5, 6, 0]


def on_device(hidden_in, cotangent, norm_gain, *rest):
    *state, round_bits = rest
    state = [
        jnp.swapaxes(array[0, 0], 0, 1) if number % 2 == 0 else array[0, 0] for number, array in enumerate(state)
    ]
    a, b = state[:2]
    h, q = hidden_in[0], cotangent[0]
    x, n, af, bf = products(h, q, norm_gain, a, b)
    gd, gu = chain(x, n, af, bf, h, q)
    named = [jnp.any(round_bits == bit).astype(jnp.int32) for bit in (1, 2, 3)]
    mask = named[0] + 2 * named[1] + 4 * named[2]
    case = jnp.sum(jnp.where(jnp.arange(8) == mask, jnp.array(CASE_OF_MASK), 0))
    out = lax.switch(case, [make_update(bits, i) for i, bits in enumerate(CASES)], gd, gu, norm_gain, *state)
    parts = [out[RANK * k : RANK * k + RANK] for k in range(6)]
    return tuple((jnp.swapaxes(p, 0, 1) if k % 2 == 0 else p)[None, None] for k, p in enumerate(parts))


def solution(mesh):
    held = P("section", "peer", None, None)
    return jax.shard_map(
        on_device,
        mesh=mesh,
        in_specs=(P("peer", None, "section"), P("peer", None, "section"), P("section", None)) + (held,) * 6 + (P(),),
        out_specs=(held,) * 6,
        check_vma=False,
    )
```

time: 1060 us -> 157 us (0.15)
  the two profiles are of different devices: /device:TPU:2 before, /device:TPU:129 now
where the time goes in v1:
time: 157 us
  Pallas kernels  148 us (94%)
  between operations  3.35 us (2%)
  local copies, waits for them, and re-layouts  2.86 us (2%)
  other arithmetic  2.63 us (2%)
    pallas_call x1, Pallas kernels, update(): pl.pallas_call(kernel, out_shape=jax.ShapeDtypeStruct((6 * RANK, WIDTH),...  89.7 us
    pallas_call x1, Pallas kernels, products(): pl.pallas_call(products_kernel, out_shape=(jax.ShapeDtypeStruct((ALL, XW)...  52 us
    pallas_call x1, Pallas kernels, chain(): pl.pallas_call(chain_kernel, out_shape=(jax.ShapeDtypeStruct((ALL, SLICE)...  6.16 us

profile of v1, /device:TPU:129, one launch (start us, length us, event | category | flops | bytes accessed | tf_op | source)
XLA Modules:
  0.0 157.0 jit_solution(16979579762646198354)
XLA Ops:
  0.6 0.0 copy-start.8
  0.6 1.3 compare_reduce_fusion
  3.9 1.3 fusion
  5.9 0.0 copy-start
  5.9 0.8 copy-done
  6.7 0.0 copy-start.1
  6.7 0.8 copy-done.1
  7.6 0.0 copy-start.2
  7.6 0.0 copy-start.3
  7.6 0.0 copy-start.4
  7.6 0.0 copy-start.5
  7.6 0.0 copy-start.6
  7.6 0.0 copy-start.7
  7.6 52.0 %products.1 = (bf16[512,896]{1,0:T(8,128)(2,1)S(1)}, f32[8,128]{1,0:T(8,128)S(1)}, bf16[512,256]{1,0:T(8,128)(2,1)S(1)}, bf16[512,256]{1,0:T(8,128)(2,1)S(1)}) custom-call(bf16[128,256]{1,0:T(8,128)(2,1)S(1)} %bitcast.44, bf16[128,256]{1,0:T(8,128)(2,1)S(1)} %bitcast.46, f32[1,4096]{1,0:T(1,128)} %g_ref.1, bf16[32,4096]{1,0:T(8,128)(2,1)} %bitcast.48, ...), custom_call_target="tpu_custom_call" | custom-call | tf_op jit(solution)/shard_map/products/pallas_call | solution.py:140
  59.6 6.2 %chain.1 = (bf16[512,256]{1,0:T(8,128)(2,1)S(1)}, bf16[512,256]{1,0:T(8,128)(2,1)S(1)}) custom-call(bf16[512,896]{1,0:T(8,128)(2,1)S(1)} %get-tuple-element.209.x_ref, f32[8,128]{1,0:T(8,128)S(1)} %get-tuple-element.210.n_ref, bf16[512,256]{1,0:T(8,128)(2,1)S(1)} %get-tuple-element.211.af_ref, bf16[512,256]{1,0:T(8,128)(2,1)S(1)} %get-tuple-element.212.bf_ref, ...), custom_call_target="tpu_custom_call" | custom-call | tf_op jit(solution)/shard_map/chain/pallas_call | solution.py:216
  65.8 0.0 copy-done.8
  65.8 0.0 copy-done.2
  65.8 0.0 copy-done.3
  65.8 0.0 copy-done.4
  65.8 0.0 copy-done.5
  65.8 0.0 copy-done.6
  65.8 0.0 copy-done.7
  65.9 90.0 %conditional.1 = (bf16[192,4096]{1,0:T(8,128)(2,1)S(1)}) conditional(s32[]{:T(128)} %clamp.3, (bf16[512,256]{1,0:T(8,128)(2,1)S(1)}, bf16[512,256]{1,0:T(8,128)(2,1)S(1)}, f32[1,4096]{1,0:T(1,128)S(1)}, bf16[32,4096]{1,0:T(8,128)(2,1)S(1)}, bf16[32,4096]{1,0:T(8,128)(2,1)S(1)}, ...), branch_computations={%region_4.5_spmd, %region_5.6_spmd, %region_6.7_spmd, %region_7.8_... | conditional | bytes 8 | solution.py:349
  65.9 89.7 %update_3.1 = bf16[192,4096]{1,0:T(8,128)(2,1)S(1)} custom-call(bf16[512,256]{1,0:T(8,128)(2,1)S(1)} %get-tuple-element.161.gd_ref, bf16[512,256]{1,0:T(8,128)(2,1)S(1)} %get-tuple-element.162.gu_ref, f32[1,4096]{1,0:T(1,128)S(1)} %get-tuple-element.163.g_ref, bf16[32,4096]{1,0:T(8,128)(2,1)S(1)} %get-tuple-element.164.a_ref, ...), custom_call_target="tpu_custom_call" | custom-call | tf_op jit(solution)/shard_map/cond/branch_3_fun/update_3/pallas_call | solution.py:314
  155.8 1.2 slice_bitcast_fusion
Async XLA Ops:
  0.6 65.2 %copy-start.8 = (f32[1,4096]{1,0:T(1,128)S(1)}, f32[1,4096]{1,0:T(1,128)}, u32[]{:S(2)}) copy-start(f32[1,4096]{1,0:T(1,128)} %g_ref.1) | copy-start | bytes 49156
  5.9 0.8 copy-start
  6.7 0.8 copy-start.1
  7.6 58.2 %copy-start.2 = (bf16[1,1,4096,32]{2,3,1,0:T(8,128)(2,1)S(1)}, bf16[1,1,4096,32]{2,3,1,0:T(8,128)(2,1)}, u32[]{:S(2)}) copy-start(bf16[1,1,4096,32]{2,3,1,0:T(8,128)(2,1)} %param.21) | copy-start | bytes 786436
  7.6 58.2 %copy-start.3 = (bf16[1,1,32,4096]{3,2,1,0:T(8,128)(2,1)S(1)}, bf16[1,1,32,4096]{3,2,1,0:T(8,128)(2,1)}, u32[]{:S(2)}) copy-start(bf16[1,1,32,4096]{3,2,1,0:T(8,128)(2,1)} %param.22) | copy-start | bytes 786436
  7.6 58.2 %copy-start.4 = (bf16[1,1,4096,32]{2,3,1,0:T(8,128)(2,1)S(1)}, bf16[1,1,4096,32]{2,3,1,0:T(8,128)(2,1)}, u32[]{:S(2)}) copy-start(bf16[1,1,4096,32]{2,3,1,0:T(8,128)(2,1)} %param.23) | copy-start | bytes 786436
  7.6 58.3 %copy-start.5 = (bf16[1,1,32,4096]{3,2,1,0:T(8,128)(2,1)S(1)}, bf16[1,1,32,4096]{3,2,1,0:T(8,128)(2,1)}, u32[]{:S(2)}) copy-start(bf16[1,1,32,4096]{3,2,1,0:T(8,128)(2,1)} %param.24) | copy-start | bytes 786436
  7.6 58.3 %copy-start.6 = (bf16[1,1,4096,32]{2,3,1,0:T(8,128)(2,1)S(1)}, bf16[1,1,4096,32]{2,3,1,0:T(8,128)(2,1)}, u32[]{:S(2)}) copy-start(bf16[1,1,4096,32]{2,3,1,0:T(8,128)(2,1)} %param.25) | copy-start | bytes 786436
  7.6 58.3 %copy-start.7 = (bf16[1,1,32,4096]{3,2,1,0:T(8,128)(2,1)S(1)}, bf16[1,1,32,4096]{3,2,1,0:T(8,128)(2,1)}, u32[]{:S(2)}) copy-start(bf16[1,1,32,4096]{3,2,1,0:T(8,128)(2,1)} %param.26) | copy-start | bytes 786436

commit v2 on v1

--- a/solution.py
+++ b/solution.py
@@ -165,7 +165,7 @@
     )(h, q, gain, a, b)
 
 
-def chain_kernel(x_ref, n_ref, af_ref, bf_ref, h_ref, q_ref, gd_ref, gu_ref, xt, lat, scaled_inner, cl, wp, rms):
+def run_chain(x_ref, n_ref, af_ref, bf_ref, h_ref, q_ref, gd_ref, gu_ref, xt, lat, scaled_inner, cl, wp, rms):
     rs = RANK**-0.5
     xt[...] = x_ref[:, 0:ALL].astype(F32).T.astype(BF16)
 
@@ -212,23 +212,16 @@
     gu_ref[...] = (up * rs).astype(BF16)
 
 
-def chain(x, n, af, bf, h, q):
-    return pl.pallas_call(
-        chain_kernel,
-        out_shape=(jax.ShapeDtypeStruct((ALL, SLICE), BF16),) * 2,
-        in_specs=[VMEM] * 6,
-        out_specs=(VMEM,) * 2,
-        scratch_shapes=[
-            pltpu.VMEM((ALL, ALL), BF16),
-            pltpu.VMEM((ALL, TOKENS), BF16),
-            pltpu.VMEM((ALL, TOKENS), BF16),
-            pltpu.VMEM((ALL, TOKENS), BF16),
-            pltpu.VMEM((ALL, TOKENS), F32),
-            pltpu.VMEM((SECTIONS, TOKENS), F32),
-        ],
-        compiler_params=pltpu.CompilerParams(vmem_limit_bytes=LIMIT),
-        name="chain",
-    )(x, n, af, bf, h, q)
+CHAIN_SCRATCH = [
+    pltpu.VMEM((ALL, SLICE), BF16),
+    pltpu.VMEM((ALL, SLICE), BF16),
+    pltpu.VMEM((ALL, ALL), BF16),
+    pltpu.VMEM((ALL, TOKENS), BF16),
+    pltpu.VMEM((ALL, TOKENS), BF16),
+    pltpu.VMEM((ALL, TOKENS), BF16),
+    pltpu.VMEM((ALL, TOKENS), F32),
+    pltpu.VMEM((SECTIONS, TOKENS), F32),
+]
 
 
 def adam(param, first, second, grad):
@@ -241,97 +234,218 @@
 
 
 def make_update(bits, number):
-    near = tuple(b for b in bits if b != 4)
-    steps = [(b, "split") for b in near] + [(4, "swap")] + [(b, "join") for b in reversed(near)]
-    widths = {b: WIDTH >> (i + 1) for i, b in enumerate(near)}
-    widths[4] = WIDTH >> len(near)
-
-    def kernel(gd_ref, gu_ref, g_ref, a_ref, b_ref, ma_ref, mb_ref, va_ref, vb_ref, out, work, gdf, gup, sd, rd, su, ru, ss, sr, *landing):
+    zbits = tuple(b for b in bits if b not in (0, 4))
+    group = 1 << len(zbits)
+    offsets = [sum(1 << b for i, b in enumerate(zbits) if m >> i & 1) for m in range(group)]
+    half_width = WIDTH // 2
+    first = 0 if not zbits else 1280 if zbits == (1,) else 1024
+    za = first // group
+    yb_width = (half_width - first) // 2
+    zb = yb_width // group
+
+    def kernel(
+        x_ref, n_ref, af_ref, bf_ref, h_ref, q_ref, g_ref, *rest
+    ):
+        state, out, rest = rest[:6], rest[6], rest[7:]
+        gd, gu, xt, lat, scaled_inner, cl, wp, rms = rest[:8]
+        work, half, gdf, gup, landc, sd, rd, su, ru, sc, rc, sj, rj = rest[8:21]
+        rest = rest[21:]
         me, peer = lax.axis_index("section"), lax.axis_index("peer")
-        land = dict(zip(near + (4,), landing))
+        core, far = peer % 2, peer // 16
+        rank = sum(((peer // (1 << b)) % 2) * (1 << i) for i, b in enumerate(zbits)) if zbits else 0
+
         barrier = pltpu.get_barrier_semaphore()
         for j in range(1, SECTIONS):
             pl.semaphore_signal(barrier, inc=1, device_id=((me + j) % SECTIONS, peer), device_id_type=MESH)
-        for b in bits:
-            pl.semaphore_signal(barrier, inc=1, device_id=(me, peer ^ (1 << b)), device_id_type=MESH)
-        pl.semaphore_wait(barrier, SECTIONS - 1 + len(bits))
+        partners = [1, 16] + offsets[1:]
+        for offset in partners:
+            pl.semaphore_signal(barrier, inc=1, device_id=(me, peer ^ offset), device_id_type=MESH)
+        run_chain(x_ref, n_ref, af_ref, bf_ref, h_ref, q_ref, gd, gu, xt, lat, scaled_inner, cl, wp, rms)
+        pl.semaphore_wait(barrier, SECTIONS - 1 + len(partners))
 
         mine = pl.ds(pl.multiple_of(me * SLICE, SLICE), SLICE)
-        copies = []
+        sends = []
         for j in range(1, SECTIONS):
             to = (me + j) % SECTIONS
             rows = pl.ds(pl.multiple_of(to * RANK, RANK), RANK)
-            copies.append(remote(gd_ref.at[rows], gdf.at[:, mine], sd.at[j], rd.at[j], to, peer))
-            copies.append(remote(gu_ref.at[rows], gup.at[:, mine], su.at[j], ru.at[j], to, peer))
-        for copy in copies:
+            sends.append(remote(gd.at[rows], gdf.at[:, mine], sd.at[j], rd.at[me], to, peer))
+            sends.append(remote(gu.at[rows], gup.at[:, mine], su.at[j], ru.at[me], to, peer))
+        for copy in sends:
             copy.start()
         rows = pl.ds(pl.multiple_of(me * RANK, RANK), RANK)
-        gdf[:, mine] = gd_ref[rows, :]
-        gup[:, mine] = gu_ref[rows, :]
-        for copy in copies:
-            copy.wait()
-
-        def step(i, _):
-            cols = pl.ds(pl.multiple_of(i * 512, 512), 512)
+        gdf[:, mine] = gd[rows, :]
+        gup[:, mine] = gu[rows, :]
+
+        def advance(f):
+            cols = pl.ds(pl.multiple_of(f * SLICE, SLICE), SLICE)
+
+            @pl.when(f != me)
+            def _():
+                remote(gd.at[0:RANK], gdf.at[:, cols], sd.at[0], rd.at[f], me, peer).wait_recv()
+                remote(gu.at[0:RANK], gup.at[:, cols], su.at[0], ru.at[f], me, peer).wait_recv()
+
+            a_ref, b_ref, ma_ref, mb_ref, va_ref, vb_ref = state
             grad = gdf[:, cols].astype(F32) * g_ref[:, cols]
             new = adam(a_ref[:, cols], ma_ref[:, cols], va_ref[:, cols], grad)
             other = adam(b_ref[:, cols], mb_ref[:, cols], vb_ref[:, cols], gup[:, cols].astype(F32))
             for k, value in enumerate((new[0], other[0], new[1], other[1], new[2], other[2])):
                 work[RANK * k : RANK * k + RANK, cols] = value.astype(BF16)
+            return cols
+
+        def core_copy(k):
+            cols = pl.ds(pl.multiple_of(((1 - core) * 8 + k) * SLICE, SLICE), SLICE)
+            there = pl.ds(pl.multiple_of(k * SLICE, SLICE), SLICE)
+            return remote(work.at[:, cols], landc.at[:, there], sc.at[k], rc.at[k], me, peer ^ 1)
+
+        def give(i, _):
+            k = (me + i) % 8
+            advance((1 - core) * 8 + k)
+            core_copy(k).start()
             return 0
 
-        lax.fori_loop(0, WIDTH // 512, step, 0)
-
-        start = 0
-        for number_of, (b, kind) in enumerate(steps):
-            bit = (peer // (1 << b)) % 2
-            to = peer + (1 - 2 * bit) * (1 << b)
-            width = widths[b]
-            if kind == "split":
-                keep = pl.ds(pl.multiple_of(start + bit * width, width), width)
-                give = pl.ds(pl.multiple_of(start + (1 - bit) * width, width), width)
-                copy = remote(work.at[:, give], land[b], ss.at[number_of], sr.at[number_of], me, to)
-                start = start + bit * width
-            elif kind == "swap":
-                keep = pl.ds(pl.multiple_of(start, width), width)
-                copy = remote(work.at[:, keep], land[b], ss.at[number_of], sr.at[number_of], me, to)
-            else:
-                keep = pl.ds(pl.multiple_of(start, width), width)
-                copy = remote(out.at[:, keep], out.at[:, keep], ss.at[number_of], sr.at[number_of], me, to)
-                start = start - bit * width
+        def keep(i, _):
+            k = (me + i) % 8
+            cols = advance(core * 8 + k)
+            copy = core_copy(k)
+            copy.wait_recv()
+            here = pl.ds(pl.multiple_of(k * SLICE, SLICE), SLICE)
+            half[:, here] = ((work[:, cols].astype(F32) + landc[:, here].astype(F32)) * 0.5).astype(BF16)
+            return 0
+
+        lax.fori_loop(0, 8, give, 0)
+        lax.fori_loop(0, 8, keep, 0)
+
+        def mean(*values):
+            total = values[0].astype(F32)
+            for value in values[1:]:
+                total += value.astype(F32)
+            return (total * (1.0 / len(values))).astype(BF16)
+
+        def cols_at(at, width):
+            return pl.ds(pl.multiple_of(at, 128), width)
+
+        base = core * half_width
+        pending = []
+        joins = iter(range(4))
+
+        def join(cols):
+            k = next(joins)
+            copy = remote(out.at[:, cols], out.at[:, cols], sj.at[k], rj.at[k], me, peer ^ 1)
             copy.start()
+            pending.append(copy)
+
+        if not zbits:
+            land_y, sy, ry = rest
+            parts = 4
+            width = half_width // parts
+            swaps = []
+            for k in range(parts):
+                cols = pl.ds(k * width, width)
+                copy = remote(half.at[:, cols], land_y.at[:, cols], sy.at[k], ry.at[k], me, peer ^ 16)
+                copy.start()
+                swaps.append(copy)
+            for k in range(parts):
+                cols = pl.ds(k * width, width)
+                swaps[k].wait()
+                there = cols_at(base + k * width, width)
+                out[:, there] = mean(half[:, cols], land_y[:, cols])
+                join(there)
+        else:
+            land_a, land_a2, acc_a, land_b, land_b2, acc_b, sems_s, sems_r = rest
+            count = iter(range(32))
+
+            def send(src, dst, offset):
+                k = next(count)
+                copy = remote(src, dst, sems_s.at[k], sems_r.at[k], me, peer ^ offset)
+                copy.start()
+                return copy
+
+            y_split = send(half.at[:, cols_at(first + (1 - far) * yb_width, yb_width)], land_b, 16)
+            z_split = [
+                send(half.at[:, cols_at((rank ^ m) * za, za)], land_a.at[m - 1], offsets[m]) for m in range(1, group)
+            ]
+            for copy in z_split:
+                copy.wait()
+            acc_a[...] = mean(half[:, cols_at(rank * za, za)], *[land_a[m] for m in range(group - 1)])
+            y_swap = send(acc_a, land_a2, 16)
+            y_split.wait()
+            acc_b[...] = mean(half[:, cols_at(first + far * yb_width, yb_width)], land_b[...])
+            z_swap = [
+                send(acc_b.at[:, cols_at((rank ^ m) * zb, zb)] if group > 2 else acc_b, land_b2.at[m - 1], offsets[m])
+                for m in range(1, group)
+            ]
+            b_here = cols_at(base + first + far * yb_width, yb_width)
+            b_part = cols_at(base + first + far * yb_width + rank * zb, zb) if group > 2 else b_here
+            a_part = cols_at(base + rank * za, za)
+            for copy in z_swap:
+                copy.wait()
+            own = acc_b[:, cols_at(rank * zb, zb)] if group > 2 else acc_b[...]
+            out[:, b_part] = mean(own, *[land_b2[m] for m in range(group - 1)])
+            if group > 2:
+                z_back = [send(out.at[:, b_part], out.at[:, b_part], offsets[m]) for m in range(1, group)]
+                for copy in z_back:
+                    copy.wait()
+            y_join = send(out.at[:, b_here], out.at[:, b_here], 16)
+            y_swap.wait()
+            out[:, a_part] = mean(acc_a[...], land_a2[...])
+            z_join = [send(out.at[:, a_part], out.at[:, a_part], offsets[m]) for m in range(1, group)]
+            y_join.wait()
+            join(cols_at(base + first, half_width - first))
+            for copy in z_join:
+                copy.wait()
+            join(cols_at(base, first))
+        for copy in pending:
             copy.wait()
-            if kind != "join":
-                mean = ((work[:, keep].astype(F32) + land[b][...].astype(F32)) * 0.5).astype(BF16)
-                if kind == "split":
-                    work[:, keep] = mean
-                else:
-                    out[:, keep] = mean
+        for copy in sends:
+            copy.wait_send()
+
+        def sent(k, _):
+            core_copy(k).wait_send()
+            return 0
+
+        lax.fori_loop(0, 8, sent, 0)
 
     dma = pltpu.SemaphoreType.DMA
-
-    def update(gd, gu, gain, *state):
+    rows = 6 * RANK
+    scratch = CHAIN_SCRATCH + [
+        pltpu.VMEM((rows, WIDTH), BF16),
+        pltpu.VMEM((rows, half_width), BF16),
+        pltpu.VMEM((RANK, WIDTH), BF16),
+        pltpu.VMEM((RANK, WIDTH), BF16),
+        pltpu.VMEM((rows, half_width), BF16),
+    ]
+    scratch += [dma((SECTIONS,))] * 4 + [dma((8,))] * 2 + [dma((4,))] * 2
+    if not zbits:
+        scratch += [pltpu.VMEM((rows, half_width), BF16), dma((4,)), dma((4,))]
+    else:
+        scratch += [
+            pltpu.VMEM((group - 1, rows, za), BF16),
+            pltpu.VMEM((rows, za), BF16),
+            pltpu.VMEM((rows, za), BF16),
+            pltpu.VMEM((rows, yb_width), BF16),
+            pltpu.VMEM((group - 1, rows, zb if group > 2 else yb_width), BF16),
+            pltpu.VMEM((rows, yb_width), BF16),
+            dma((16,)),
+            dma((16,)),
+        ]
+
+    def update(*operands):
         return pl.pallas_call(
             kernel,
-            out_shape=jax.ShapeDtypeStruct((6 * RANK, WIDTH), BF16),
-            in_specs=[VMEM] * 9,
+            out_shape=jax.ShapeDtypeStruct((rows, WIDTH), BF16),
+            in_specs=[VMEM] * 13,
             out_specs=VMEM,
-            scratch_shapes=[pltpu.VMEM((6 * RANK, WIDTH), BF16)]
-            + [pltpu.VMEM((RANK, WIDTH), BF16)] * 2
-            + [dma((SECTIONS,))] * 4
-            + [dma((len(steps),))] * 2
-            + [pltpu.VMEM((6 * RANK, widths[b]), BF16) for b in near + (4,)],
+            scratch_shapes=scratch,
             compiler_params=pltpu.CompilerParams(
                 collective_id=1 + number, has_side_effects=True, vmem_limit_bytes=LIMIT
             ),
             name=f"update_{number}",
-        )(gd, gu, gain, *state)
+        )(*operands)
 
     return update
 
 
-CASES = [(0, 4), (0, 1, 4), (0, 2, 4), (0, 3, 4), (0, 1, 2, 4), (0, 1, 3, 4), (0, 2, 3, 4)]
-CASE_OF_MASK = [0, 1, 2, 4, 3, 5, 6, 0]
+CASES = [(0, 4), (0, 1, 4), (0, 2, 4), (0, 1, 2, 4), (0, 3, 4), (0, 1, 3, 4), (0, 2, 3, 4)]
 
 
 def on_device(hidden_in, cotangent, norm_gain, *rest):
@@ -342,11 +456,10 @@
     a, b = state[:2]
     h, q = hidden_in[0], cotangent[0]
     x, n, af, bf = products(h, q, norm_gain, a, b)
-    gd, gu = chain(x, n, af, bf, h, q)
-    named = [jnp.any(round_bits == bit).astype(jnp.int32) for bit in (1, 2, 3)]
-    mask = named[0] + 2 * named[1] + 4 * named[2]
-    case = jnp.sum(jnp.where(jnp.arange(8) == mask, jnp.array(CASE_OF_MASK), 0))
-    out = lax.switch(case, [make_update(bits, i) for i, bits in enumerate(CASES)], gd, gu, norm_gain, *state)
+    mask = lax.reduce(jnp.left_shift(jnp.int32(1), round_bits), jnp.int32(0), lax.bitwise_or, (0,))
+    case = jnp.bitwise_and(jnp.right_shift(mask, 1), 7)
+    branches = [make_update(bits, i) for i, bits in enumerate(CASES)]
+    out = lax.switch(case, branches, x, n, af, bf, h, q, norm_gain, *state)
     parts = [out[RANK * k : RANK * k + RANK] for k in range(6)]
     return tuple((jnp.swapaxes(p, 0, 1) if k % 2 == 0 else p)[None, None] for k, p in enumerate(parts))
 

time: 157 us -> 118 us (0.75)
  the two profiles are of different devices: /device:TPU:129 before, /device:TPU:325 now
where the time goes in v2:
time: 118 us
  Pallas kernels  114 us (97%)
  between operations  1.3 us (1%)
  other arithmetic  1.29 us (1%)
    pallas_call x1, Pallas kernels, update(): pl.pallas_call(kernel, out_shape=jax.ShapeDtypeStruct((rows, WIDTH), BF16...  61.1 us
    pallas_call x1, Pallas kernels, products(): pl.pallas_call(products_kernel, out_shape=(jax.ShapeDtypeStruct((ALL, XW)...  52.5 us

profile of v2, /device:TPU:325, one launch (start us, length us, event | category | flops | bytes accessed | tf_op | source)
XLA Modules:
  0.0 118.0 jit_solution(10415260674894925512)
XLA Ops:
  0.6 1.3 %shift-left_reduce_fusion = s32[]{:T(128)} fusion(s32[4]{0:T(128)} %param.26), kind=kLoop, calls=%fused_computation.6 | loop fusion | flops 7 | bytes 20 | tf_op jit(solution)/shard_map/reduce | solution.py:459
  2.6 52.5 %products.1 = (bf16[512,896]{1,0:T(8,128)(2,1)S(1)}, f32[8,128]{1,0:T(8,128)S(1)}, bf16[512,256]{1,0:T(8,128)(2,1)S(1)}, bf16[512,256]{1,0:T(8,128)(2,1)S(1)}) custom-call(bf16[128,256]{1,0:T(8,128)(2,1)} %bitcast.76, bf16[128,256]{1,0:T(8,128)(2,1)} %bitcast.84, f32[1,4096]{1,0:T(1,128)} %g_ref.1, bf16[32,4096]{1,0:T(8,128)(2,1)} %bitcast.32, ...), custom_call_target="tpu_custom_call" | custom-call | tf_op jit(solution)/shard_map/products/pallas_call | solution.py:140
  55.0 61.8 %conditional.1 = (bf16[192,4096]{1,0:T(8,128)(2,1)S(1)}) conditional(s32[]{:T(128)} %clamp.3, (bf16[512,896]{1,0:T(8,128)(2,1)S(1)}, f32[8,128]{1,0:T(8,128)S(1)}, bf16[512,256]{1,0:T(8,128)(2,1)S(1)}, bf16[512,256]{1,0:T(8,128)(2,1)S(1)}, bf16[128,256]{1,0:T(8,128)(2,1)}, /*index=5*/bf16[128,256]{1,0:T(8,128)(2,1)}, ...), branch_computations={%region_1.0_spmd, %region_2.0_spmd, %region_3.0_spmd, %region_4.0_... | conditional | bytes 8 | solution.py:462
  55.1 61.1 %update_1.1 = bf16[192,4096]{1,0:T(8,128)(2,1)S(1)} custom-call(bf16[512,896]{1,0:T(8,128)(2,1)S(1)} %get-tuple-element.203.x_ref, f32[8,128]{1,0:T(8,128)S(1)} %get-tuple-element.204.n_ref, bf16[512,256]{1,0:T(8,128)(2,1)S(1)} %get-tuple-element.205.af_ref, bf16[512,256]{1,0:T(8,128)(2,1)S(1)} %get-tuple-element.206.bf_ref, ...), custom_call_target="tpu_custom_call" | custom-call | tf_op jit(solution)/shard_map/cond/branch_1_fun/update_1/pallas_call | solution.py:433
  116.9 1.2 slice_bitcast_fusion

commit v3 on v2

--- a/solution.py
+++ b/solution.py
@@ -36,9 +36,12 @@
     )
 
 
+CHUNKS = ((ALL + TOKENS, 2 * TOKENS), (ALL // 2, ALL // 2 + TOKENS), (0, ALL // 2))
+
+
 def products_kernel(
     h_ref, q_ref, g_ref, a_ref, b_ref, x_ref, n_ref, af_ref, bf_ref,
-    scaled, part, rx, px, ry, npart, nrx, npx, nry, sa, ra, sb, rb, sx, rxs, sn, rn, sy, rys, sm, rm, sg, rg, sh, rh,
+    scaled, part, rx, px, ry, npart, nrx, npx, nry, sa, ra, sb, rb, sx, rxs, sy, rys, sg, rg, sh, rh, sn, rn, sm, rm,
 ):
     me, peer = lax.axis_index("section"), lax.axis_index("peer")
     mx, my = me // NY, me % NY
@@ -50,14 +53,19 @@
     pl.semaphore_wait(barrier, SECTIONS - 1)
 
     mine = pl.ds(pl.multiple_of(me * RANK, RANK), RANK)
-    copies = []
-    for j in range(1, SECTIONS):
-        to = (me + j) % SECTIONS
-        cols = pl.ds(pl.multiple_of(to * SLICE, SLICE), SLICE)
-        copies.append(remote(scaled.at[:, cols], af_ref.at[mine], sa.at[j], ra.at[j], to, peer))
-        copies.append(remote(b_ref.at[:, cols], bf_ref.at[mine], sb.at[j], rb.at[j], to, peer))
-    for copy in copies:
-        copy.start()
+
+    def scatter(src, dst, send, recv):
+        copies = []
+        for j in range(1, SECTIONS):
+            to = (me + j) % SECTIONS
+            cols = pl.ds(pl.multiple_of(to * SLICE, SLICE), SLICE)
+            copies.append(remote(src.at[:, cols], dst.at[mine], send.at[j], recv.at[j], to, peer))
+        for copy in copies:
+            copy.start()
+        return copies
+
+    b_copies = scatter(b_ref, bf_ref, sb, rb)
+    a_copies = scatter(scaled, af_ref, sa, ra)
     cols = pl.ds(pl.multiple_of(me * SLICE, SLICE), SLICE)
     af_ref[mine, :] = scaled[:, cols]
     bf_ref[mine, :] = b_ref[:, cols]
@@ -67,71 +75,112 @@
     low = (square - high.astype(F32)).astype(BF16)
     ones = jnp.ones((8, SLICE), BF16)
     npart[...] = dot(ones, high, NT) + dot(ones, low, NT)
-    for copy in copies:
+    rs = RANK**-0.5
+
+    def group_rows(x):
+        return pl.ds(pl.multiple_of(x * NY * RANK, NY * RANK), NY * RANK)
+
+    def rank_rows(y):
+        return pl.ds(pl.multiple_of(y * RANK, RANK), RANK)
+
+    held = [pl.ds(at, width) for at, width in CHUNKS]
+    flying = [None] * len(CHUNKS)
+
+    def started(copies):
+        for copy in copies:
+            copy.start()
+        return copies
+
+    def landed(c):
+        for copy in flying[c]:
+            copy.wait()
+
+    def reduce_x(c):
+        copies = []
+        for j in range(1, NX):
+            x, k = (mx + j) % NX, 4 * c + j
+            to = x * NY + my
+            copies.append(remote(part.at[group_rows(x), held[c]], rx.at[j - 1, :, held[c]], sx.at[k], rxs.at[k], to, peer))
+            if c == 0:
+                copies.append(remote(npart, nrx.at[j - 1], sn.at[j], rn.at[j], to, peer))
+        flying[c] = started(copies)
+
+    def reduce_y(c):
+        landed(c)
+        total = part[group_rows(mx), held[c]].astype(F32)
+        for j in range(NX - 1):
+            total += rx[j, :, held[c]].astype(F32)
+        px[:, held[c]] = total.astype(BF16)
+        if c == 0:
+            npx[...] = npart[...] + nrx[0] + nrx[1] + nrx[2]
+        copies = []
+        for j in range(1, NY):
+            y, k = (my + j) % NY, 4 * c + j
+            to = mx * NY + y
+            copies.append(remote(px.at[rank_rows(y), held[c]], ry.at[j - 1, :, held[c]], sy.at[k], rys.at[k], to, peer))
+            if c == 0:
+                copies.append(remote(npx, nry.at[j - 1], sm.at[j], rm.at[j], to, peer))
+        flying[c] = started(copies)
+
+    def gather_y(c):
+        landed(c)
+        total = px[rank_rows(my), held[c]].astype(F32)
+        for j in range(NY - 1):
+            total += ry[j, :, held[c]].astype(F32)
+        x_ref[mine, held[c]] = total.astype(BF16)
+        if c == 0:
+            n_ref[...] = npx[...] + nry[0] + nry[1] + nry[2]
+        rows = x_ref.at[mine, held[c]]
+        flying[c] = started(
+            [
+                remote(rows, rows, sg.at[4 * c + j], rg.at[4 * c + j], mx * NY + (my + j) % NY, peer)
+                for j in range(1, NY)
+            ]
+        )
+
+    def gather_x(c):
+        landed(c)
+        rows = x_ref.at[group_rows(mx), held[c]]
+        flying[c] = started(
+            [
+                remote(rows, rows, sh.at[4 * c + j], rh.at[4 * c + j], ((mx + j) % NX) * NY + my, peer)
+                for j in range(1, NX)
+            ]
+        )
+
+    for copy in b_copies:
         copy.wait()
-
-    af, bf = af_ref[...], bf_ref[...]
-    rs = RANK**-0.5
-    lower, _ = block_masks()
-    part[:, 0:ALL] = jnp.where(lower, dot(af, bf, NT) * rs, dot(bf, bf, NT) * (1.0 / RANK)).astype(BF16)
-    part[:, ALL : ALL + TOKENS] = dot(af, h, NT).astype(BF16)
+    bf = bf_ref[...]
     part[:, ALL + TOKENS : ALL + 2 * TOKENS] = (dot(bf, h, NT) * rs).astype(BF16)
     part[:, ALL + 2 * TOKENS : XW] = (dot(bf, q_ref[...], NT) * rs).astype(BF16)
-
-    group = NY * RANK
-
-    def group_rows(x):
-        return pl.ds(pl.multiple_of(x * group, group), group)
-
-    copies = []
-    for j in range(1, NX):
-        x = (mx + j) % NX
-        copies.append(remote(part.at[group_rows(x)], rx.at[j - 1], sx.at[j], rxs.at[j], x * NY + my, peer))
-        copies.append(remote(npart, nrx.at[j - 1], sn.at[j], rn.at[j], x * NY + my, peer))
-    for copy in copies:
-        copy.start()
-    for copy in copies:
+    reduce_x(0)
+    for copy in a_copies:
         copy.wait()
-    total = part[group_rows(mx), :].astype(F32)
-    for j in range(NX - 1):
-        total += rx[j].astype(F32)
-    px[...] = total.astype(BF16)
-    npx[...] = npart[...] + nrx[0] + nrx[1] + nrx[2]
-
-    def rank_rows(y):
-        return pl.ds(pl.multiple_of(y * RANK, RANK), RANK)
-
-    copies = []
-    for j in range(1, NY):
-        y = (my + j) % NY
-        copies.append(remote(px.at[rank_rows(y)], ry.at[j - 1], sy.at[j], rys.at[j], mx * NY + y, peer))
-        copies.append(remote(npx, nry.at[j - 1], sm.at[j], rm.at[j], mx * NY + y, peer))
-    for copy in copies:
-        copy.start()
-    for copy in copies:
-        copy.wait()
-    total = px[rank_rows(my), :].astype(F32)
-    for j in range(NY - 1):
-        total += ry[j].astype(F32)
-    x_ref[mine, :] = total.astype(BF16)
-    n_ref[...] = npx[...] + nry[0] + nry[1] + nry[2]
-
-    copies = []
-    for j in range(1, NY):
-        to = mx * NY + (my + j) % NY
-        copies.append(remote(x_ref.at[mine], x_ref.at[mine], sg.at[j], rg.at[j], to, peer))
-    for copy in copies:
-        copy.start()
-    for copy in copies:
-        copy.wait()
-    copies = []
-    for j in range(1, NX):
-        to = ((mx + j) % NX) * NY + my
-        copies.append(remote(x_ref.at[group_rows(mx)], x_ref.at[group_rows(mx)], sh.at[j], rh.at[j], to, peer))
-    for copy in copies:
-        copy.start()
-    for copy in copies:
-        copy.wait()
+    af = af_ref[...]
+    lower, _ = block_masks()
+
+    def squares(at):
+        other = bf_ref[at : at + ALL // 2, :]
+        mask = lower[:, at : at + ALL // 2]
+        products = jnp.where(mask, dot(af, other, NT) * rs, dot(bf, other, NT) * (1.0 / RANK))
+        part[:, at : at + ALL // 2] = products.astype(BF16)
+
+    part[:, ALL : ALL + TOKENS] = dot(af, h, NT).astype(BF16)
+    squares(ALL // 2)
+    reduce_x(1)
+    squares(0)
+    reduce_x(2)
+    reduce_y(0)
+    reduce_y(1)
+    gather_y(0)
+    reduce_y(2)
+    gather_y(1)
+    gather_x(0)
+    gather_y(2)
+    gather_x(1)
+    gather_x(2)
+    for c in range(len(CHUNKS)):
+        landed(c)
 
 
 def products(h, q, gain, a, b):
@@ -159,7 +208,8 @@
             pltpu.VMEM((NY - 1, 8, TOKENS), F32),
         ]
         + [dma((SECTIONS,))] * 4
-        + [dma((4,))] * 12,
+        + [dma((4 * len(CHUNKS),))] * 8
+        + [dma((4,))] * 4,
         compiler_params=pltpu.CompilerParams(collective_id=0, has_side_effects=True, vmem_limit_bytes=LIMIT),
         name="products",
     )(h, q, gain, a, b)

time: 118 us -> 114 us (0.966)
  the two profiles are of different devices: /device:TPU:325 before, /device:TPU:9 now
where the time goes in v3:
time: 114 us; the launch traced here: 113 us
  Pallas kernels  109 us (96%)
  between operations  1.3 us (1%)
  other arithmetic  1.29 us (1%)
  local copies, waits for them, and re-layouts  1.15 us (1%)
    pallas_call x1, Pallas kernels, update(): pl.pallas_call(kernel, out_shape=jax.ShapeDtypeStruct((rows, WIDTH), BF16...  62.9 us
    pallas_call x1, Pallas kernels, products(): pl.pallas_call(products_kernel, out_shape=(jax.ShapeDtypeStruct((ALL, XW)...  46.1 us

profile of v3, /device:TPU:9, one launch (start us, length us, event | category | flops | bytes accessed | tf_op | source)
XLA Modules:
  0.0 113.5 jit_solution(7099415390294117026)
XLA Ops:
  0.6 1.3 %shift-left_reduce_fusion = s32[]{:T(128)} fusion(s32[4]{0:T(128)} %param.26), kind=kLoop, calls=%fused_computation.6 | loop fusion | flops 7 | bytes 20 | tf_op jit(solution)/shard_map/reduce | solution.py:509
  2.6 46.1 %products.1 = (bf16[512,896]{1,0:T(8,128)(2,1)S(1)}, f32[8,128]{1,0:T(8,128)S(1)}, bf16[512,256]{1,0:T(8,128)(2,1)S(1)}, bf16[512,256]{1,0:T(8,128)(2,1)S(1)}) custom-call(bf16[128,256]{1,0:T(8,128)(2,1)} %bitcast.76, bf16[128,256]{1,0:T(8,128)(2,1)} %bitcast.84, f32[1,4096]{1,0:T(1,128)} %g_ref.1, bf16[32,4096]{1,0:T(8,128)(2,1)} %bitcast.32, ...), custom_call_target="tpu_custom_call" | custom-call | tf_op jit(solution)/shard_map/products/pallas_call | solution.py:189
  48.7 63.7 %conditional.1 = (bf16[192,4096]{1,0:T(8,128)(2,1)S(1)}) conditional(s32[]{:T(128)} %clamp.3, (bf16[512,896]{1,0:T(8,128)(2,1)S(1)}, f32[8,128]{1,0:T(8,128)S(1)}, bf16[512,256]{1,0:T(8,128)(2,1)S(1)}, bf16[512,256]{1,0:T(8,128)(2,1)S(1)}, bf16[128,256]{1,0:T(8,128)(2,1)}, /*index=5*/bf16[128,256]{1,0:T(8,128)(2,1)}, ...), branch_computations={%region_1.0_spmd, %region_2.0_spmd, %region_3.0_spmd, %region_4.0_... | conditional | bytes 8 | solution.py:512
  48.9 62.9 %update_2.1 = bf16[192,4096]{1,0:T(8,128)(2,1)S(1)} custom-call(bf16[512,896]{1,0:T(8,128)(2,1)S(1)} %get-tuple-element.216.x_ref, f32[8,128]{1,0:T(8,128)S(1)} %get-tuple-element.217.n_ref, bf16[512,256]{1,0:T(8,128)(2,1)S(1)} %get-tuple-element.218.af_ref, bf16[512,256]{1,0:T(8,128)(2,1)S(1)} %get-tuple-element.219.bf_ref, ...), custom_call_target="tpu_custom_call" | custom-call | tf_op jit(solution)/shard_map/cond/branch_2_fun/update_2/pallas_call | solution.py:483
  112.3 1.2 %slice_bitcast_fusion = (bf16[1,1,32,4096]{3,2,1,0:T(8,128)(2,1)}, bf16[1,1,4096,32]{2,3,1,0:T(8,128)(2,1)}, bf16[1,1,32,4096]{3,2,1,0:T(8,128)(2,1)}, bf16[1,1,...) fusion(bf16[192,4096]{1,0:T(8,128)(2,1)S(1)} %get-tuple-element.301), kind=kLoop, calls=%fused_computation | loop fusion | bytes 3145728 | tf_op jit(solution)/shard_map/broadcast_in_dim | solution.py:514

commit v4 on v3

v4 whole, which is shorter than its diff:
```python
import jax
import jax.numpy as jnp
from jax import lax
from jax.experimental import pallas as pl
from jax.experimental.pallas import tpu as pltpu
from jax.sharding import PartitionSpec as P

ADAM_STEP = 100
MESH = pl.DeviceIdType.MESH
F32, BF16 = jnp.float32, jnp.bfloat16
SECTIONS, NX, NY = 16, 4, 4
RANK, WIDTH, TOKENS = 32, 4096, 128
SLICE = WIDTH // SECTIONS
ALL = SECTIONS * RANK
XW = ALL + 3 * TOKENS
VMEM = pl.BlockSpec(memory_space=pltpu.VMEM)
SMEM = pl.BlockSpec(memory_space=pltpu.SMEM)
LIMIT = 48 << 20

NN = (((1,), (0,)), ((), ()))
NT = (((1,), (1,)), ((), ()))


def dot(a, b, dims=NN):
    return lax.dot_general(a, b, dims, preferred_element_type=F32)


def block_masks():
    row = lax.broadcasted_iota(jnp.int32, (ALL, ALL), 0) // RANK
    col = lax.broadcasted_iota(jnp.int32, (ALL, ALL), 1) // RANK
    return row > col, row < col


def remote(src, dst, send, recv, section, peer):
    return pltpu.make_async_remote_copy(
        src_ref=src, dst_ref=dst, send_sem=send, recv_sem=recv, device_id=(section, peer), device_id_type=MESH
    )


CHUNKS = ((ALL + TOKENS, 2 * TOKENS), (ALL // 2, ALL // 2 + TOKENS), (0, ALL // 2))


def products_kernel(
    bits_ref, h_hbm, q_hbm, g_hbm, a_hbm, b_hbm, case_ref, x_ref, n_ref, af_ref, bf_ref,
    h_ref, q_ref, g_ref, a_ref, b_ref, loaded, scaled, part, rx, px, ry, npart, nrx, npx, nry, sa, ra, sb, rb, sx, rxs, sy, rys, sg, rg, sh, rh, sn, rn, sm, rm,
):
    me, peer = lax.axis_index("section"), lax.axis_index("peer")
    mx, my = me // NY, me % NY

    operands = [(a_hbm, a_ref), (g_hbm, g_ref), (b_hbm, b_ref), (h_hbm, h_ref), (q_hbm, q_ref)]
    loads = [pltpu.make_async_copy(src, dst, loaded.at[k]) for k, (src, dst) in enumerate(operands)]
    for load in loads:
        load.start()
    barrier = pltpu.get_barrier_semaphore()
    for j in range(1, SECTIONS):
        pl.semaphore_signal(barrier, inc=1, device_id=((me + j) % SECTIONS, peer), device_id_type=MESH)
    case_ref[0] = sum(
        jnp.maximum(
            jnp.maximum((bits_ref[0] == bit).astype(jnp.int32), (bits_ref[1] == bit).astype(jnp.int32)),
            jnp.maximum((bits_ref[2] == bit).astype(jnp.int32), (bits_ref[3] == bit).astype(jnp.int32)),
        )
        << (bit - 1)
        for bit in (1, 2, 3)
    )
    for load in loads:
        load.wait()
    scaled[...] = (a_ref[...].astype(F32) * (g_ref[...] * WIDTH**-0.5)).astype(BF16)
    pl.semaphore_wait(barrier, SECTIONS - 1)

    mine = pl.ds(pl.multiple_of(me * RANK, RANK), RANK)

    def scatter(src, dst, send, recv):
        copies = []
        for j in range(1, SECTIONS):
            to = (me + j) % SECTIONS
            cols = pl.ds(pl.multiple_of(to * SLICE, SLICE), SLICE)
            copies.append(remote(src.at[:, cols], dst.at[mine], send.at[j], recv.at[j], to, peer))
        for copy in copies:
            copy.start()
        return copies

    b_copies = scatter(b_ref, bf_ref, sb, rb)
    a_copies = scatter(scaled, af_ref, sa, ra)
    cols = pl.ds(pl.multiple_of(me * SLICE, SLICE), SLICE)
    af_ref[mine, :] = scaled[:, cols]
    bf_ref[mine, :] = b_ref[:, cols]
    h = h_ref[...]
    square = h.astype(F32) * h.astype(F32)
    high = square.astype(BF16)
    low = (square - high.astype(F32)).astype(BF16)
    ones = jnp.ones((8, SLICE), BF16)
    npart[...] = dot(ones, high, NT) + dot(ones, low, NT)
    rs = RANK**-0.5

    def group_rows(x):
        return pl.ds(pl.multiple_of(x * NY * RANK, NY * RANK), NY * RANK)

    def rank_rows(y):
        return pl.ds(pl.multiple_of(y * RANK, RANK), RANK)

    held = [pl.ds(at, width) for at, width in CHUNKS]
    flying = [None] * len(CHUNKS)

    def started(copies):
        for copy in copies:
            copy.start()
        return copies

    def landed(c):
        for copy in flying[c]:
            copy.wait()

    def reduce_x(c):
        copies = []
        for j in range(1, NX):
            x, k = (mx + j) % NX, 4 * c + j
            to = x * NY + my
            copies.append(remote(part.at[group_rows(x), held[c]], rx.at[j - 1, :, held[c]], sx.at[k], rxs.at[k], to, peer))
            if c == 0:
                copies.append(remote(npart, nrx.at[j - 1], sn.at[j], rn.at[j], to, peer))
        flying[c] = started(copies)

    def reduce_y(c):
        landed(c)
        total = part[group_rows(mx), held[c]].astype(F32)
        for j in range(NX - 1):
            total += rx[j, :, held[c]].astype(F32)
        px[:, held[c]] = total.astype(BF16)
        if c == 0:
            npx[...] = npart[...] + nrx[0] + nrx[1] + nrx[2]
        copies = []
        for j in range(1, NY):
            y, k = (my + j) % NY, 4 * c + j
            to = mx * NY + y
            copies.append(remote(px.at[rank_rows(y), held[c]], ry.at[j - 1, :, held[c]], sy.at[k], rys.at[k], to, peer))
            if c == 0:
                copies.append(remote(npx, nry.at[j - 1], sm.at[j], rm.at[j], to, peer))
        flying[c] = started(copies)

    def gather_y(c):
        landed(c)
        total = px[rank_rows(my), held[c]].astype(F32)
        for j in range(NY - 1):
            total += ry[j, :, held[c]].astype(F32)
        x_ref[mine, held[c]] = total.astype(BF16)
        if c == 0:
            n_ref[...] = npx[...] + nry[0] + nry[1] + nry[2]
        rows = x_ref.at[mine, held[c]]
        flying[c] = started(
            [
                remote(rows, rows, sg.at[4 * c + j], rg.at[4 * c + j], mx * NY + (my + j) % NY, peer)
                for j in range(1, NY)
            ]
        )

    def gather_x(c):
        landed(c)
        rows = x_ref.at[group_rows(mx), held[c]]
        flying[c] = started(
            [
                remote(rows, rows, sh.at[4 * c + j], rh.at[4 * c + j], ((mx + j) % NX) * NY + my, peer)
                for j in range(1, NX)
            ]
        )

    for copy in b_copies:
        copy.wait()
    bf = bf_ref[...]
    part[:, ALL + TOKENS : ALL + 2 * TOKENS] = (dot(bf, h, NT) * rs).astype(BF16)
    part[:, ALL + 2 * TOKENS : XW] = (dot(bf, q_ref[...], NT) * rs).astype(BF16)
    reduce_x(0)
    for copy in a_copies:
        copy.wait()
    af = af_ref[...]
    lower, _ = block_masks()

    def squares(at):
        other = bf_ref[at : at + ALL // 2, :]
        mask = lower[:, at : at + ALL // 2]
        products = jnp.where(mask, dot(af, other, NT) * rs, dot(bf, other, NT) * (1.0 / RANK))
        part[:, at : at + ALL // 2] = products.astype(BF16)

    part[:, ALL : ALL + TOKENS] = dot(af, h, NT).astype(BF16)
    squares(ALL // 2)
    reduce_x(1)
    squares(0)
    reduce_x(2)
    reduce_y(0)
    reduce_y(1)
    gather_y(0)
    reduce_y(2)
    gather_y(1)
    gather_x(0)
    gather_y(2)
    gather_x(1)
    gather_x(2)
    for c in range(len(CHUNKS)):
        landed(c)


def products(bits, h, q, gain, a, b):
    dma = pltpu.SemaphoreType.DMA
    group = NY * RANK
    return pl.pallas_call(
        products_kernel,
        out_shape=(
            jax.ShapeDtypeStruct((1,), jnp.int32),
            jax.ShapeDtypeStruct((ALL, XW), BF16),
            jax.ShapeDtypeStruct((8, TOKENS), F32),
            jax.ShapeDtypeStruct((ALL, SLICE), BF16),
            jax.ShapeDtypeStruct((ALL, SLICE), BF16),
        ),
        in_specs=[SMEM] + [pl.BlockSpec(memory_space=pl.ANY)] * 5,
        out_specs=(SMEM,) + (VMEM,) * 4,
        scratch_shapes=[
            pltpu.VMEM((TOKENS, SLICE), BF16),
            pltpu.VMEM((TOKENS, SLICE), BF16),
            pltpu.VMEM((1, WIDTH), F32),
            pltpu.VMEM((RANK, WIDTH), BF16),
            pltpu.VMEM((RANK, WIDTH), BF16),
            dma((5,)),
            pltpu.VMEM((RANK, WIDTH), BF16),
            pltpu.VMEM((ALL, XW), BF16),
            pltpu.VMEM((NX - 1, group, XW), BF16),
            pltpu.VMEM((group, XW), BF16),
            pltpu.VMEM((NY - 1, RANK, XW), BF16),
            pltpu.VMEM((8, TOKENS), F32),
            pltpu.VMEM((NX - 1, 8, TOKENS), F32),
            pltpu.VMEM((8, TOKENS), F32),
            pltpu.VMEM((NY - 1, 8, TOKENS), F32),
        ]
        + [dma((SECTIONS,))] * 4
        + [dma((4 * len(CHUNKS),))] * 8
        + [dma((4,))] * 4,
        compiler_params=pltpu.CompilerParams(collective_id=0, has_side_effects=True, vmem_limit_bytes=LIMIT),
        name="products",
    )(bits, h, q, gain, a, b)


def rows_of(s):
    return slice(RANK * s, RANK * s + RANK)


def forward(x_ref, n_ref, xt, lat, wp, rms):
    xt[...] = x_ref[:, 0:ALL].astype(F32).T.astype(BF16)
    norm = n_ref[0:1, :]
    for s in range(SECTIONS):
        rows = rows_of(s)
        u = x_ref[rows, ALL : ALL + TOKENS].astype(F32)
        w = x_ref[rows, ALL + TOKENS : ALL + 2 * TOKENS].astype(F32)
        if s > 0:
            before = lat[0 : RANK * s, :]
            u += dot(x_ref[rows, 0 : RANK * s], before)
            w += dot(xt[rows, 0 : RANK * s], before)
        r = lax.rsqrt(jnp.maximum(norm, 0.0) * (1.0 / WIDTH) + 1e-5)
        latent = (u * r).astype(BF16)
        lat[rows, :] = latent
        after = w + dot(xt[rows, rows], latent)
        norm += jnp.sum(latent.astype(F32) * (w + after), axis=0, keepdims=True)
        wp[rows, :] = after
        rms[s : s + 1, :] = r


def backward(x_ref, xt, lat, scaled_inner, cl, wp, rms):
    carry = jnp.zeros((1, TOKENS), F32)
    for s in reversed(range(SECTIONS)):
        rows = rows_of(s)
        inner = x_ref[rows, ALL + 2 * TOKENS : XW].astype(F32) - carry * wp[rows, :]
        if s < SECTIONS - 1:
            later = RANK * (s + 1)
            inner += dot(xt[rows, later:ALL], scaled_inner[later:ALL, :])
            inner -= dot(x_ref[rows, later:ALL], cl[later:ALL, :])
        r = rms[s : s + 1, :]
        latent = lat[rows, :].astype(F32)
        scaled_inner[rows, :] = (r * inner).astype(BF16)
        cl[rows, :] = (carry * latent).astype(BF16)
        carry += r * r * (jnp.sum(latent * inner, axis=0, keepdims=True) * (1.0 / WIDTH))


def down_gradient(af_ref, bf_ref, h_ref, lat, scaled_inner, gd_ref):
    lower, _ = block_masks()
    ri = scaled_inner[...]
    mixed = jnp.where(lower, dot(ri, lat[...], NT), 0.0).astype(BF16)
    down = dot(ri, h_ref[...]) + dot(mixed, bf_ref[...]) * RANK**-0.5
    gd_ref[...] = (down * WIDTH**-0.5).astype(BF16)


def up_gradient(af_ref, bf_ref, h_ref, q_ref, lat, scaled_inner, cl, gu_ref):
    _, upper = block_masks()
    rs = RANK**-0.5
    ls, ri, cls = lat[...], scaled_inner[...], cl[...]
    mixed = jnp.where(upper, dot(ls, cls, NT), dot(cls, ls, NT)).astype(BF16)
    up = dot(ls, q_ref[...]) - dot(cls, h_ref[...]) - dot(mixed, bf_ref[...]) * rs
    up += dot(jnp.where(upper, dot(ls, ri, NT), 0.0).astype(BF16), af_ref[...])
    gu_ref[...] = (up * rs).astype(BF16)


CHAIN_SCRATCH = [
    pltpu.VMEM((ALL, SLICE), BF16),
    pltpu.VMEM((ALL, SLICE), BF16),
    pltpu.VMEM((ALL, ALL), BF16),
    pltpu.VMEM((ALL, TOKENS), BF16),
    pltpu.VMEM((ALL, TOKENS), BF16),
    pltpu.VMEM((ALL, TOKENS), BF16),
    pltpu.VMEM((ALL, TOKENS), F32),
    pltpu.VMEM((SECTIONS, TOKENS), F32),
]


def adam(param, first, second, grad):
    first_new = 0.9 * first.astype(F32) + 0.1 * grad
    second_new = 0.999 * second.astype(F32) + 0.001 * grad * grad
    corr_one = 1.0 - 0.9**ADAM_STEP
    corr_two = 1.0 - 0.999**ADAM_STEP
    update = 0.05 * (first_new / corr_one) / (jnp.sqrt(second_new / corr_two) + 1e-08)
    return param.astype(F32) - update, first_new, second_new


def make_update(bits, number):
    zbits = tuple(b for b in bits if b not in (0, 4))
    group = 1 << len(zbits)
    offsets = [sum(1 << b for i, b in enumerate(zbits) if m >> i & 1) for m in range(group)]
    half_width = WIDTH // 2
    rows_each = 3 * RANK
    turn = half_width if len(zbits) == 0 or zbits == (1,) else half_width // 2

    def kernel(x_ref, n_ref, af_ref, bf_ref, h_ref, q_ref, g_ref, *rest):
        held, out, rest = rest[:6], rest[6], rest[7:]
        gd, gu, xt, lat, scaled_inner, cl, wp, rms = rest[:8]
        state, other, half, gdf, gup, sl, so, ro, sd, rd, su, ru, sj, rj = rest[8:22]
        rest = rest[22:]
        me, peer = lax.axis_index("section"), lax.axis_index("peer")
        core, far = peer % 2, peer // 16
        rank = sum(((peer // (1 << b)) % 2) * (1 << i) for i, b in enumerate(zbits)) if zbits else 0
        keeper = me // 8
        place = pl.ds(pl.multiple_of((me % 8) * SLICE, SLICE), SLICE)
        foreign = (core + keeper) % 2
        slot = foreign * 8 + me % 8

        loads = [pltpu.make_async_copy(held[k], state.at[k], sl.at[k]) for k in range(6)]
        for load in loads:
            load.start()
        barrier = pltpu.get_barrier_semaphore()

        def signal(section, to):
            pl.semaphore_signal(barrier, inc=1, device_id=(section, to), device_id_type=MESH)

        for k in range(8):
            source = core * 8 + k
            signal(source, peer + 1 - 2 * core)

            @pl.when(source != me)
            def _():
                signal(source, peer)

        partners = [1, 16] + offsets[1:]
        for offset in partners:
            signal(me, peer ^ offset)
        forward(x_ref, n_ref, xt, lat, wp, rms)
        pl.semaphore_wait(barrier, SECTIONS - 1 + foreign + len(partners))
        for load in loads:
            load.wait()
        theirs = pl.ds(pl.multiple_of((1 - core) * half_width, half_width), half_width)
        swaps = [remote(state.at[k, :, theirs], other.at[k], so.at[k], ro.at[k], me, peer ^ 1) for k in range(6)]
        for copy in swaps:
            copy.start()
        backward(x_ref, xt, lat, scaled_inner, cl, wp, rms)

        def gradient_copy(src, dst, send, recv, j):
            to = (me + j) % SECTIONS
            rows = pl.ds(pl.multiple_of(to * RANK, RANK), RANK)
            return remote(
                src.at[rows], dst.at[foreign, :, place], send.at[j], recv.at[slot], to, peer - core + keeper
            )

        def scatter(src, dst, send, recv):
            for j in range(1, SECTIONS):
                gradient_copy(src, dst, send, recv, j).start()

            @pl.when(foreign == 1)
            def _():
                gradient_copy(src, dst, send, recv, 0).start()

            @pl.when(foreign == 0)
            def _():
                dst[0, :, place] = src[pl.ds(pl.multiple_of(me * RANK, RANK), RANK), :]

        def scattered(src, dst, send, recv):
            for j in range(1, SECTIONS):
                gradient_copy(src, dst, send, recv, j).wait_send()

            @pl.when(foreign == 1)
            def _():
                gradient_copy(src, dst, send, recv, 0).wait_send()

        down_gradient(af_ref, bf_ref, h_ref, lat, scaled_inner, gd)
        scatter(gd, gdf, sd, rd)
        up_gradient(af_ref, bf_ref, h_ref, q_ref, lat, scaled_inner, cl, gu)
        scatter(gu, gup, su, ru)
        for copy in swaps:
            copy.wait()

        def adam_pairs(dst, src, recv, which, gain):
            def step(i, _):
                k = (me + i) % 8
                source = core * 8 + k
                cols = pl.ds(pl.multiple_of(source * SLICE, SLICE), SLICE)
                here = pl.ds(pl.multiple_of(k * SLICE, SLICE), SLICE)

                @pl.when(source != me)
                def _():
                    remote(src.at[0:RANK], dst.at[0, :, here], sd.at[0], recv.at[k], me, peer ^ 1).wait_recv()

                remote(src.at[0:RANK], dst.at[1, :, here], sd.at[0], recv.at[8 + k], me, peer ^ 1).wait_recv()
                grads = [dst[m, :, here].astype(F32) for m in range(2)]
                if gain:
                    grads = [grad * g_ref[:, cols] for grad in grads]
                mine = adam(*[state[2 * m + which, :, cols] for m in range(3)], grads[0])
                pair = adam(*[other[2 * m + which, :, here] for m in range(3)], grads[1])
                for m in range(3):
                    at = rows_each * which + RANK * m
                    half[at : at + RANK, here] = ((mine[m] + pair[m]) * 0.5).astype(BF16)
                return 0

            lax.fori_loop(0, 8, step, 0)

        def mean(*values):
            total = values[0].astype(F32)
            for value in values[1:]:
                total += value.astype(F32)
            return (total * (1.0 / len(values))).astype(BF16)

        def cols_at(at, width):
            return pl.ds(pl.multiple_of(at, 128), width)

        base = core * half_width
        pending = []
        count = iter(range(64))

        def send(src, dst, offset):
            k = next(count)
            copy = remote(src, dst, sj.at[k], rj.at[k], me, peer ^ offset)
            copy.start()
            return copy

        def join(rows, at, width):
            there = out.at[rows, cols_at(base + at, width)]
            pending.append(send(there, there, 1))

        down, up = slice(0, rows_each), slice(rows_each, 2 * rows_each)

        def only_y(rows, at, width, land):
            copy = send(half.at[rows, at : at + width], land, 16)
            yield
            copy.wait()
            out[rows, cols_at(base + at, width)] = mean(half[rows, at : at + width], land[...])
            join(rows, at, width)
            yield

        def z_first(rows, at, width, land_z, acc, land_y):
            part = width // group
            copies = [
                send(half.at[rows, cols_at(at + (rank ^ m) * part, part)], land_z.at[m - 1], offsets[m])
                for m in range(1, group)
            ]
            yield
            for copy in copies:
                copy.wait()
            acc[...] = mean(half[rows, cols_at(at + rank * part, part)], *[land_z[m] for m in range(group - 1)])
            copy = send(acc, land_y, 16)
            yield
            copy.wait()
            here = cols_at(base + at + rank * part, part)
            out[rows, here] = mean(acc[...], land_y[...])
            copies = [send(out.at[rows, here], out.at[rows, here], offsets[m]) for m in range(1, group)]
            yield
            for copy in copies:
                copy.wait()
            join(rows, at, width)
            yield

        def y_first(rows, at, width, land_y, acc, land_z):
            wide = width // 2
            part = wide // group
            copy = send(half.at[rows, cols_at(at + (1 - far) * wide, wide)], land_y, 16)
            yield
            copy.wait()
            acc[...] = mean(half[rows, cols_at(at + far * wide, wide)], land_y[...])
            whole = cols_at(base + at + far * wide, wide)
            if group == 2:
                copies = [send(acc, land_z.at[0], offsets[1])]
            else:
                copies = [
                    send(acc.at[:, cols_at((rank ^ m) * part, part)], land_z.at[m - 1], offsets[m])
                    for m in range(1, group)
                ]
            yield
            for copy in copies:
                copy.wait()
            if group == 2:
                out[rows, whole] = mean(acc[...], land_z[0])
            else:
                here = cols_at(base + at + far * wide + rank * part, part)
                own = acc[:, cols_at(rank * part, part)]
                out[rows, here] = mean(own, *[land_z[m] for m in range(group - 1)])
                copies = [send(out.at[rows, here], out.at[rows, here], offsets[m]) for m in range(1, group)]
                yield
                for copy in copies:
                    copy.wait()
            copy = send(out.at[rows, whole], out.at[rows, whole], 16)
            yield
            copy.wait()
            join(rows, at, width)
            yield

        if not zbits:
            quarter = half_width // 2
            first = [only_y(down, 0, quarter, rest[0]), only_y(down, quarter, quarter, rest[1])]
            second = [only_y(up, 0, quarter, rest[2]), only_y(up, quarter, quarter, rest[3])]
        else:
            first = [z_first(down, 0, half_width, *rest[0:3])]
            second = [z_first(up, 0, turn, *rest[3:6])]
            if turn < half_width:
                second = [y_first(up, turn, half_width - turn, *rest[6:9])] + second

        adam_pairs(gdf, gd, rd, 0, True)
        if zbits:
            for chunk in first:
                next(chunk)
        adam_pairs(gup, gu, ru, 1, False)
        for chunk in second if zbits else first + second:
            next(chunk)
        chunks = first + second
        while chunks:
            chunks = [chunk for chunk in chunks if next(chunk, "end") != "end"]
        for copy in pending:
            copy.wait()
        scattered(gd, gdf, sd, rd)
        scattered(gu, gup, su, ru)

    dma = pltpu.SemaphoreType.DMA

    def blocks(*shape):
        return pltpu.VMEM(shape, BF16)

    scratch = CHAIN_SCRATCH + [
        blocks(6, RANK, WIDTH),
        blocks(6, RANK, half_width),
        blocks(6 * RANK, half_width),
        blocks(2, RANK, half_width),
        blocks(2, RANK, half_width),
    ]
    scratch += [dma((6,))] * 3 + [dma((SECTIONS,))] * 4 + [dma((32,))] * 2
    if not zbits:
        scratch += [blocks(rows_each, half_width // 2)] * 4
    else:
        for width in (half_width, turn):
            part = width // group
            scratch += [blocks(group - 1, rows_each, part), blocks(rows_each, part), blocks(rows_each, part)]
        if turn < half_width:
            wide = (half_width - turn) // 2
            part = wide if group == 2 else wide // group
            scratch += [blocks(rows_each, wide), blocks(rows_each, wide), blocks(group - 1, rows_each, part)]

    def update(*operands):
        return pl.pallas_call(
            kernel,
            out_shape=jax.ShapeDtypeStruct((6 * RANK, WIDTH), BF16),
            in_specs=[VMEM] * 7 + [pl.BlockSpec(memory_space=pl.ANY)] * 6,
            out_specs=VMEM,
            scratch_shapes=scratch,
            compiler_params=pltpu.CompilerParams(
                collective_id=1 + number, has_side_effects=True, vmem_limit_bytes=LIMIT
            ),
            name=f"update_{number}",
        )(*operands)

    return update


CASES = [(0, 4), (0, 1, 4), (0, 2, 4), (0, 1, 2, 4), (0, 3, 4), (0, 1, 3, 4), (0, 2, 3, 4)]


def on_device(hidden_in, cotangent, norm_gain, *rest):
    *state, round_bits = rest
    state = [
        jnp.swapaxes(array[0, 0], 0, 1) if number % 2 == 0 else array[0, 0] for number, array in enumerate(state)
    ]
    a, b = state[:2]
    h, q = hidden_in[0], cotangent[0]
    case, x, n, af, bf = products(round_bits, h, q, norm_gain, a, b)
    branches = [make_update(bits, i) for i, bits in enumerate(CASES)]
    out = lax.switch(case[0], branches, x, n, af, bf, h, q, norm_gain, *state)
    parts = [out[RANK * k : RANK * k + RANK] for k in (0, 3, 1, 4, 2, 5)]
    return tuple((jnp.swapaxes(p, 0, 1) if k % 2 == 0 else p)[None, None] for k, p in enumerate(parts))


def solution(mesh):
    held = P("section", "peer", None, None)
    return jax.shard_map(
        on_device,
        mesh=mesh,
        in_specs=(P("peer", None, "section"), P("peer", None, "section"), P("section", None)) + (held,) * 6 + (P(),),
        out_specs=(held,) * 6,
        check_vma=False,
    )
```

time: 114 us -> 118 us (1.035)
  the two profiles are of different devices: /device:TPU:9 before, /device:TPU:137 now
where the time goes in v4:
time: 118 us
  Pallas kernels  114 us (97%)
  local copies, waits for them, and re-layouts  1.8 us (2%)
  between operations  1.29 us (1%)
    pallas_call x1, Pallas kernels, update(): pl.pallas_call(kernel, out_shape=jax.ShapeDtypeStruct((6 * RANK, WIDTH),...  67.9 us
    pallas_call x1, Pallas kernels, products(): pl.pallas_call(products_kernel, out_shape=(jax.ShapeDtypeStruct((1,), jnp...  45.9 us

profile of v4, /device:TPU:137, one launch (start us, length us, event | category | flops | bytes accessed | tf_op | source)
XLA Modules:
  0.0 117.7 jit_solution(12631780029406274532)
XLA Ops:
  0.6 0.0 copy-start
  0.6 0.6 copy-done
  1.3 45.9 %products.1 = (s32[1]{0:T(128)}, bf16[512,896]{1,0:T(8,128)(2,1)S(1)}, f32[8,128]{1,0:T(8,128)S(1)}, bf16[512,256]{1,0:T(8,128)(2,1)S(1)}, bf16[512,256]{1,0:T(8,128)(2,1)S(1)}) custom-call(s32[4]{0:T(128)S(1)} %copy-done, bf16[128,256]{1,0:T(8,128)(2,1)} %bitcast.77, bf16[128,256]{1,0:T(8,128)(2,1)} %bitcast.85, f32[1,4096]{1,0:T(1,128)} %g_hbm.1, ...), custom_call_target="tpu_custom_call" | custom-call | tf_op jit(solution)/shard_map/products/pallas_call | solution.py:204
  47.8 68.7 %conditional.1 = (bf16[192,4096]{1,0:T(8,128)(2,1)S(1)}) conditional(s32[]{:T(128)} %bitcast.5, (bf16[512,896]{1,0:T(8,128)(2,1)S(1)}, f32[8,128]{1,0:T(8,128)S(1)}, bf16[512,256]{1,0:T(8,128)(2,1)S(1)}, bf16[512,256]{1,0:T(8,128)(2,1)S(1)}, bf16[128,256]{1,0:T(8,128)(2,1)}, /*index=5*/bf16[128,256]{1,0:T(8,128)(2,1)}, ...), branch_computations={%region_0.0_spmd, %region_1.0_spmd, %region_2.0_spmd, %region_3.0_... | conditional | bytes 8 | solution.py:593
  48.1 67.9 %update_5.1 = bf16[192,4096]{1,0:T(8,128)(2,1)S(1)} custom-call(bf16[512,896]{1,0:T(8,128)(2,1)S(1)} %get-tuple-element.255.x_ref, f32[8,128]{1,0:T(8,128)S(1)} %get-tuple-element.256.n_ref, bf16[512,256]{1,0:T(8,128)(2,1)S(1)} %get-tuple-element.257.af_ref, bf16[512,256]{1,0:T(8,128)(2,1)S(1)} %get-tuple-element.258.bf_ref, ...), custom_call_target="tpu_custom_call" | custom-call | tf_op jit(solution)/shard_map/cond/branch_5_fun/update_5/pallas_call | solution.py:566
  116.5 1.2 slice_bitcast_fusion
Async XLA Ops:
  0.6 0.7 copy-start

commit v5 on v4

--- a/solution.py
+++ b/solution.py
@@ -13,6 +13,7 @@
 SLICE = WIDTH // SECTIONS
 ALL = SECTIONS * RANK
 XW = ALL + 3 * TOKENS
+SQ, WS, ZS = TOKENS, TOKENS + ALL, 2 * TOKENS + ALL
 VMEM = pl.BlockSpec(memory_space=pltpu.VMEM)
 SMEM = pl.BlockSpec(memory_space=pltpu.SMEM)
 LIMIT = 48 << 20
@@ -37,23 +38,25 @@
     )
 
 
-CHUNKS = ((ALL + TOKENS, 2 * TOKENS), (ALL // 2, ALL // 2 + TOKENS), (0, ALL // 2))
+CHUNKS = ((WS, 2 * TOKENS), (0, SQ + ALL // 2), (SQ + ALL // 2, ALL // 2))
 
 
 def products_kernel(
-    bits_ref, h_hbm, q_hbm, g_hbm, a_hbm, b_hbm, case_ref, x_ref, n_ref, af_ref, bf_ref,
-    h_ref, q_ref, g_ref, a_ref, b_ref, loaded, scaled, part, rx, px, ry, npart, nrx, npx, nry, sa, ra, sb, rb, sx, rxs, sy, rys, sg, rg, sh, rh, sn, rn, sm, rm,
+    bits_hbm, h_hbm, q_hbm, g_hbm, a_hbm, b_hbm, case_ref, x_ref, af_ref, bf_ref, xt, lat, wp, rms,
+    bits_ref, h_ref, q_ref, g_ref, a_ref, b_ref, loaded, n_ref, scaled, part, rx, px, ry, npart, nrx, npx, nry, sa, ra, sb, rb, sx, rxs, sy, rys, sg, rg, sh, rh, sn, rn, sm, rm,
 ):
     me, peer = lax.axis_index("section"), lax.axis_index("peer")
     mx, my = me // NY, me % NY
 
-    operands = [(a_hbm, a_ref), (g_hbm, g_ref), (b_hbm, b_ref), (h_hbm, h_ref), (q_hbm, q_ref)]
+    operands = [(a_hbm, a_ref), (g_hbm, g_ref), (b_hbm, b_ref), (h_hbm, h_ref), (q_hbm, q_ref), (bits_hbm, bits_ref)]
     loads = [pltpu.make_async_copy(src, dst, loaded.at[k]) for k, (src, dst) in enumerate(operands)]
     for load in loads:
         load.start()
     barrier = pltpu.get_barrier_semaphore()
     for j in range(1, SECTIONS):
         pl.semaphore_signal(barrier, inc=1, device_id=((me + j) % SECTIONS, peer), device_id_type=MESH)
+    for load in loads:
+        load.wait()
     case_ref[0] = sum(
         jnp.maximum(
             jnp.maximum((bits_ref[0] == bit).astype(jnp.int32), (bits_ref[1] == bit).astype(jnp.int32)),
@@ -62,8 +65,6 @@
         << (bit - 1)
         for bit in (1, 2, 3)
     )
-    for load in loads:
-        load.wait()
     scaled[...] = (a_ref[...].astype(F32) * (g_ref[...] * WIDTH**-0.5)).astype(BF16)
     pl.semaphore_wait(barrier, SECTIONS - 1)
 
@@ -166,8 +167,8 @@
     for copy in b_copies:
         copy.wait()
     bf = bf_ref[...]
-    part[:, ALL + TOKENS : ALL + 2 * TOKENS] = (dot(bf, h, NT) * rs).astype(BF16)
-    part[:, ALL + 2 * TOKENS : XW] = (dot(bf, q_ref[...], NT) * rs).astype(BF16)
+    part[:, WS:ZS] = (dot(bf, h, NT) * rs).astype(BF16)
+    part[:, ZS:XW] = (dot(bf, q_ref[...], NT) * rs).astype(BF16)
     reduce_x(0)
     for copy in a_copies:
         copy.wait()
@@ -178,12 +179,12 @@
         other = bf_ref[at : at + ALL // 2, :]
         mask = lower[:, at : at + ALL // 2]
         products = jnp.where(mask, dot(af, other, NT) * rs, dot(bf, other, NT) * (1.0 / RANK))
-        part[:, at : at + ALL // 2] = products.astype(BF16)
-
-    part[:, ALL : ALL + TOKENS] = dot(af, h, NT).astype(BF16)
+        part[:, SQ + at : SQ + at + ALL // 2] = products.astype(BF16)
+
+    part[:, 0:SQ] = dot(af, h, NT).astype(BF16)
+    squares(0)
+    reduce_x(1)
     squares(ALL // 2)
-    reduce_x(1)
-    squares(0)
     reduce_x(2)
     reduce_y(0)
     reduce_y(1)
@@ -194,8 +195,11 @@
     gather_y(2)
     gather_x(1)
     gather_x(2)
-    for c in range(len(CHUNKS)):
-        landed(c)
+    landed(0)
+    landed(1)
+    norm = forward(range(SECTIONS // 2), n_ref[0:1, :], x_ref, xt, lat, wp, rms)
+    landed(2)
+    forward(range(SECTIONS // 2, SECTIONS), norm, x_ref, xt, lat, wp, rms)
 
 
 def products(bits, h, q, gain, a, b):
@@ -206,19 +210,24 @@
         out_shape=(
             jax.ShapeDtypeStruct((1,), jnp.int32),
             jax.ShapeDtypeStruct((ALL, XW), BF16),
-            jax.ShapeDtypeStruct((8, TOKENS), F32),
             jax.ShapeDtypeStruct((ALL, SLICE), BF16),
             jax.ShapeDtypeStruct((ALL, SLICE), BF16),
+            jax.ShapeDtypeStruct((ALL, ALL), BF16),
+            jax.ShapeDtypeStruct((ALL, TOKENS), BF16),
+            jax.ShapeDtypeStruct((ALL, TOKENS), F32),
+            jax.ShapeDtypeStruct((SECTIONS, TOKENS), F32),
         ),
-        in_specs=[SMEM] + [pl.BlockSpec(memory_space=pl.ANY)] * 5,
-        out_specs=(SMEM,) + (VMEM,) * 4,
+        in_specs=[pl.BlockSpec(memory_space=pl.ANY)] * 6,
+        out_specs=(SMEM,) + (VMEM,) * 7,
         scratch_shapes=[
+            pltpu.SMEM((4,), jnp.int32),
             pltpu.VMEM((TOKENS, SLICE), BF16),
             pltpu.VMEM((TOKENS, SLICE), BF16),
             pltpu.VMEM((1, WIDTH), F32),
             pltpu.VMEM((RANK, WIDTH), BF16),
             pltpu.VMEM((RANK, WIDTH), BF16),
-            dma((5,)),
+            dma((6,)),
+            pltpu.VMEM((8, TOKENS), F32),
             pltpu.VMEM((RANK, WIDTH), BF16),
             pltpu.VMEM((ALL, XW), BF16),
             pltpu.VMEM((NX - 1, group, XW), BF16),
@@ -241,16 +250,16 @@
     return slice(RANK * s, RANK * s + RANK)
 
 
-def forward(x_ref, n_ref, xt, lat, wp, rms):
-    xt[...] = x_ref[:, 0:ALL].astype(F32).T.astype(BF16)
-    norm = n_ref[0:1, :]
-    for s in range(SECTIONS):
+def forward(sections, norm, x_ref, xt, lat, wp, rms):
+    half = slice(RANK * sections[0], RANK * sections[-1] + RANK)
+    xt[half, :] = x_ref[:, SQ + half.start : SQ + half.stop].astype(F32).T.astype(BF16)
+    for s in sections:
         rows = rows_of(s)
-        u = x_ref[rows, ALL : ALL + TOKENS].astype(F32)
-        w = x_ref[rows, ALL + TOKENS : ALL + 2 * TOKENS].astype(F32)
+        u = x_ref[rows, 0:SQ].astype(F32)
+        w = x_ref[rows, WS:ZS].astype(F32)
         if s > 0:
             before = lat[0 : RANK * s, :]
-            u += dot(x_ref[rows, 0 : RANK * s], before)
+            u += dot(x_ref[rows, SQ : SQ + RANK * s], before)
             w += dot(xt[rows, 0 : RANK * s], before)
         r = lax.rsqrt(jnp.maximum(norm, 0.0) * (1.0 / WIDTH) + 1e-5)
         latent = (u * r).astype(BF16)
@@ -259,17 +268,18 @@
         norm += jnp.sum(latent.astype(F32) * (w + after), axis=0, keepdims=True)
         wp[rows, :] = after
         rms[s : s + 1, :] = r
+    return norm
 
 
 def backward(x_ref, xt, lat, scaled_inner, cl, wp, rms):
     carry = jnp.zeros((1, TOKENS), F32)
     for s in reversed(range(SECTIONS)):
         rows = rows_of(s)
-        inner = x_ref[rows, ALL + 2 * TOKENS : XW].astype(F32) - carry * wp[rows, :]
+        inner = x_ref[rows, ZS:XW].astype(F32) - carry * wp[rows, :]
         if s < SECTIONS - 1:
             later = RANK * (s + 1)
             inner += dot(xt[rows, later:ALL], scaled_inner[later:ALL, :])
-            inner -= dot(x_ref[rows, later:ALL], cl[later:ALL, :])
+            inner -= dot(x_ref[rows, SQ + later : SQ + ALL], cl[later:ALL, :])
         r = rms[s : s + 1, :]
         latent = lat[rows, :].astype(F32)
         scaled_inner[rows, :] = (r * inner).astype(BF16)
@@ -298,12 +308,8 @@
 CHAIN_SCRATCH = [
     pltpu.VMEM((ALL, SLICE), BF16),
     pltpu.VMEM((ALL, SLICE), BF16),
-    pltpu.VMEM((ALL, ALL), BF16),
     pltpu.VMEM((ALL, TOKENS), BF16),
     pltpu.VMEM((ALL, TOKENS), BF16),
-    pltpu.VMEM((ALL, TOKENS), BF16),
-    pltpu.VMEM((ALL, TOKENS), F32),
-    pltpu.VMEM((SECTIONS, TOKENS), F32),
 ]
 
 
@@ -322,13 +328,13 @@
     offsets = [sum(1 << b for i, b in enumerate(zbits) if m >> i & 1) for m in range(group)]
     half_width = WIDTH // 2
     rows_each = 3 * RANK
-    turn = half_width if len(zbits) == 0 or zbits == (1,) else half_width // 2
-
-    def kernel(x_ref, n_ref, af_ref, bf_ref, h_ref, q_ref, g_ref, *rest):
-        held, out, rest = rest[:6], rest[6], rest[7:]
-        gd, gu, xt, lat, scaled_inner, cl, wp, rms = rest[:8]
-        state, other, half, gdf, gup, sl, so, ro, sd, rd, su, ru, sj, rj = rest[8:22]
-        rest = rest[22:]
+    turn = {(): half_width, (2,): 512, (3,): 512, (1, 2): half_width}.get(zbits, half_width // 2)
+
+    def kernel(x_ref, af_ref, bf_ref, xt, lat, wp, rms, h_ref, q_ref, g_ref, *rest):
+        held, outs, rest = rest[:6], rest[6:8], rest[8:]
+        gd, gu, scaled_inner, cl = rest[:4]
+        state, other, half, gdf, gup, sl, so, ro, sd, rd, su, ru, sj, rj = rest[4:18]
+        rest = rest[18:]
         me, peer = lax.axis_index("section"), lax.axis_index("peer")
         core, far = peer % 2, peer // 16
         rank = sum(((peer // (1 << b)) % 2) * (1 << i) for i, b in enumerate(zbits)) if zbits else 0
@@ -356,45 +362,44 @@
         partners = [1, 16] + offsets[1:]
         for offset in partners:
             signal(me, peer ^ offset)
-        forward(x_ref, n_ref, xt, lat, wp, rms)
+        backward(x_ref, xt, lat, scaled_inner, cl, wp, rms)
+        down_gradient(af_ref, bf_ref, h_ref, lat, scaled_inner, gd)
         pl.semaphore_wait(barrier, SECTIONS - 1 + foreign + len(partners))
+
+        def gradient_copy(src, dst, send, recv, j):
+            to = (me + j) % SECTIONS
+            rows = pl.ds(pl.multiple_of(to * RANK, RANK), RANK)
+            return remote(
+                src.at[rows], dst.at[foreign, :, place], send.at[j], recv.at[slot], to, peer - core + keeper
+            )
+
+        def scatter(src, dst, send, recv):
+            for j in range(1, SECTIONS):
+                gradient_copy(src, dst, send, recv, j).start()
+
+            @pl.when(foreign == 1)
+            def _():
+                gradient_copy(src, dst, send, recv, 0).start()
+
+            @pl.when(foreign == 0)
+            def _():
+                dst[0, :, place] = src[pl.ds(pl.multiple_of(me * RANK, RANK), RANK), :]
+
+        def scattered(src, dst, send, recv):
+            for j in range(1, SECTIONS):
+                gradient_copy(src, dst, send, recv, j).wait_send()
+
+            @pl.when(foreign == 1)
+            def _():
+                gradient_copy(src, dst, send, recv, 0).wait_send()
+
+        scatter(gd, gdf, sd, rd)
         for load in loads:
             load.wait()
         theirs = pl.ds(pl.multiple_of((1 - core) * half_width, half_width), half_width)
         swaps = [remote(state.at[k, :, theirs], other.at[k], so.at[k], ro.at[k], me, peer ^ 1) for k in range(6)]
         for copy in swaps:
             copy.start()
-        backward(x_ref, xt, lat, scaled_inner, cl, wp, rms)
-
-        def gradient_copy(src, dst, send, recv, j):
-            to = (me + j) % SECTIONS
-            rows = pl.ds(pl.multiple_of(to * RANK, RANK), RANK)
-            return remote(
-                src.at[rows], dst.at[foreign, :, place], send.at[j], recv.at[slot], to, peer - core + keeper
-            )
-
-        def scatter(src, dst, send, recv):
-            for j in range(1, SECTIONS):
-                gradient_copy(src, dst, send, recv, j).start()
-
-            @pl.when(foreign == 1)
-            def _():
-                gradient_copy(src, dst, send, recv, 0).start()
-
-            @pl.when(foreign == 0)
-            def _():
-                dst[0, :, place] = src[pl.ds(pl.multiple_of(me * RANK, RANK), RANK), :]
-
-        def scattered(src, dst, send, recv):
-            for j in range(1, SECTIONS):
-                gradient_copy(src, dst, send, recv, j).wait_send()
-
-            @pl.when(foreign == 1)
-            def _():
-                gradient_copy(src, dst, send, recv, 0).wait_send()
-
-        down_gradient(af_ref, bf_ref, h_ref, lat, scaled_inner, gd)
-        scatter(gd, gdf, sd, rd)
         up_gradient(af_ref, bf_ref, h_ref, q_ref, lat, scaled_inner, cl, gu)
         scatter(gu, gup, su, ru)
         for copy in swaps:
@@ -443,8 +448,11 @@
             copy.start()
             return copy
 
+        def out(rows):
+            return outs[0] if rows.start == 0 else outs[1]
+
         def join(rows, at, width):
-            there = out.at[rows, cols_at(base + at, width)]
+            there = out(rows).at[:, cols_at(base + at, width)]
             pending.append(send(there, there, 1))
 
         down, up = slice(0, rows_each), slice(rows_each, 2 * rows_each)
@@ -453,7 +461,7 @@
             copy = send(half.at[rows, at : at + width], land, 16)
             yield
             copy.wait()
-            out[rows, cols_at(base + at, width)] = mean(half[rows, at : at + width], land[...])
+            out(rows)[:, cols_at(base + at, width)] = mean(half[rows, at : at + width], land[...])
             join(rows, at, width)
             yield
 
@@ -471,8 +479,8 @@
             yield
             copy.wait()
             here = cols_at(base + at + rank * part, part)
-            out[rows, here] = mean(acc[...], land_y[...])
-            copies = [send(out.at[rows, here], out.at[rows, here], offsets[m]) for m in range(1, group)]
+            out(rows)[:, here] = mean(acc[...], land_y[...])
+            copies = [send(out(rows).at[:, here], out(rows).at[:, here], offsets[m]) for m in range(1, group)]
             yield
             for copy in copies:
                 copy.wait()
@@ -498,16 +506,16 @@
             for copy in copies:
                 copy.wait()
             if group == 2:
-                out[rows, whole] = mean(acc[...], land_z[0])
+                out(rows)[:, whole] = mean(acc[...], land_z[0])
             else:
                 here = cols_at(base + at + far * wide + rank * part, part)
                 own = acc[:, cols_at(rank * part, part)]
-                out[rows, here] = mean(own, *[land_z[m] for m in range(group - 1)])
-                copies = [send(out.at[rows, here], out.at[rows, here], offsets[m]) for m in range(1, group)]
+                out(rows)[:, here] = mean(own, *[land_z[m] for m in range(group - 1)])
+                copies = [send(out(rows).at[:, here], out(rows).at[:, here], offsets[m]) for m in range(1, group)]
                 yield
                 for copy in copies:
                     copy.wait()
-            copy = send(out.at[rows, whole], out.at[rows, whole], 16)
+            copy = send(out(rows).at[:, whole], out(rows).at[:, whole], 16)
             yield
             copy.wait()
             join(rows, at, width)
@@ -519,9 +527,11 @@
             second = [only_y(up, 0, quarter, rest[2]), only_y(up, quarter, quarter, rest[3])]
         else:
             first = [z_first(down, 0, half_width, *rest[0:3])]
-            second = [z_first(up, 0, turn, *rest[3:6])]
+            second = []
             if turn < half_width:
-                second = [y_first(up, turn, half_width - turn, *rest[6:9])] + second
+                second.append(y_first(up, turn, half_width - turn, *rest[-3:]))
+            if turn > 0:
+                second.append(z_first(up, 0, turn, *rest[3:6]))
 
         adam_pairs(gdf, gd, rd, 0, True)
         if zbits:
@@ -554,7 +564,7 @@
     if not zbits:
         scratch += [blocks(rows_each, half_width // 2)] * 4
     else:
-        for width in (half_width, turn):
+        for width in (half_width, turn) if turn else (half_width,):
             part = width // group
             scratch += [blocks(group - 1, rows_each, part), blocks(rows_each, part), blocks(rows_each, part)]
         if turn < half_width:
@@ -565,9 +575,9 @@
     def update(*operands):
         return pl.pallas_call(
             kernel,
-            out_shape=jax.ShapeDtypeStruct((6 * RANK, WIDTH), BF16),
-            in_specs=[VMEM] * 7 + [pl.BlockSpec(memory_space=pl.ANY)] * 6,
-            out_specs=VMEM,
+            out_shape=(jax.ShapeDtypeStruct((rows_each, WIDTH), BF16),) * 2,
+            in_specs=[VMEM] * 10 + [pl.BlockSpec(memory_space=pl.ANY)] * 6,
+            out_specs=(VMEM,) * 2,
             scratch_shapes=scratch,
             compiler_params=pltpu.CompilerParams(
                 collective_id=1 + number, has_side_effects=True, vmem_limit_bytes=LIMIT
@@ -588,10 +598,10 @@
     ]
     a, b = state[:2]
     h, q = hidden_in[0], cotangent[0]
-    case, x, n, af, bf = products(round_bits, h, q, norm_gain, a, b)
+    case, *chain = products(round_bits, h, q, norm_gain, a, b)
     branches = [make_update(bits, i) for i, bits in enumerate(CASES)]
-    out = lax.switch(case[0], branches, x, n, af, bf, h, q, norm_gain, *state)
-    parts = [out[RANK * k : RANK * k + RANK] for k in (0, 3, 1, 4, 2, 5)]
+    out = lax.switch(case[0], branches, *chain, h, q, norm_gain, *state)
+    parts = [out[k % 2][RANK * (k // 2) : RANK * (k // 2) + RANK] for k in range(6)]
     return tuple((jnp.swapaxes(p, 0, 1) if k % 2 == 0 else p)[None, None] for k, p in enumerate(parts))
 
 

time: 118 us -> 108 us (0.915)
  the two profiles are of different devices: /device:TPU:137 before, /device:TPU:31 now
where the time goes in v5:
time: 108 us
  Pallas kernels  104 us (96%)
  local copies, waits for them, and re-layouts  1.92 us (2%)
  between operations  1.42 us (1%)
    pallas_call x1, Pallas kernels, update(): pl.pallas_call(kernel, out_shape=(jax.ShapeDtypeStruct((rows_each, WIDTH)...  62.9 us
    pallas_call x1, Pallas kernels, products(): pl.pallas_call(products_kernel, out_shape=(jax.ShapeDtypeStruct((1,), jnp...  41.5 us

profile of v5, /device:TPU:31, one launch (start us, length us, event | category | flops | bytes accessed | tf_op | source)
XLA Modules:
  0.0 108.2 jit_solution(16803994832102194991)
XLA Ops:
  0.6 0.0 copy-start
  0.6 0.6 copy-done
  1.3 0.0 copy-start.1
  1.3 0.0 copy-start.2
  1.3 0.0 copy-start.3
  1.3 0.0 copy-start.4
  1.3 41.5 %products.1 = (s32[1]{0:T(128)}, bf16[512,896]{1,0:T(8,128)(2,1)S(1)}, bf16[512,256]{1,0:T(8,128)(2,1)S(1)}, bf16[512,256]{1,0:T(8,128)(2,1)S(1)}, bf16[512,512]...) custom-call(s32[4]{0:T(128)S(1)} %copy-done, ...), custom_call_target="tpu_custom_call" | custom-call | tf_op jit(solution)/shard_map/products/pallas_call | solution.py:208
  42.8 0.0 copy-start.5
  43.4 0.0 copy-done.1
  43.4 0.0 copy-done.2
  43.4 0.0 copy-done.3
  43.5 0.0 copy-done.4
  43.5 0.1 copy-done.5
  43.5 63.4 %conditional.1 = (bf16[96,4096]{1,0:T(8,128)(2,1)S(1)}, bf16[1,1,32,4096]{3,2,1,0:T(8,128)(2,1)S(1)}, bf16[1,1,32,4096]{3,2,1,0:T(8,128)(2,1)S(1)}, bf16[1,1,32,4096]{3,2,1,0:T(8,128)(2,1)S(1)}) conditional(s32[]{:T(128)} %bitcast.5, (bf16[512,896]{1,0:T(8,128)(2,1)S(1)}, bf16[512,256]{1,0:T(8,128)(2,1)S(1)}, ...), branch_computations={%region_0.0_spmd.clone.clone, %region_1.0_spmd.clone.clone, %regio... | conditional | bytes 1572896 | solution.py:603
  43.7 62.9 %update_3.3 = (bf16[96,4096]{1,0:T(8,128)(2,1)S(1)}, bf16[96,4096]{1,0:T(8,128)(2,1)S(1)}) custom-call(bf16[512,896]{1,0:T(8,128)(2,1)S(1)} %get-tuple-element.689.x_ref, bf16[512,256]{1,0:T(8,128)(2,1)S(1)} %get-tuple-element.690.af_ref, bf16[512,256]{1,0:T(8,128)(2,1)S(1)} %get-tuple-element.691.bf_ref, bf16[512,512]{1,0:T(8,128)(2,1)S(1)} %get-tuple-element.692.xt, ...), custom_call_target="tpu_custom_call" | custom-call | tf_op jit(solution)/shard_map/cond/branch_3_fun/update_3/pallas_call | solution.py:576
  106.6 0.1 slice_bitcast_fusion.9
  107.0 0.0 copy-start.6
  107.0 0.0 copy-start.7
  107.0 0.0 copy-start.8
  107.0 1.0 slice_bitcast_fusion.21
  108.0 0.0 copy-done.6
  108.0 0.0 copy-done.7
  108.0 0.1 copy-done.8
Async XLA Ops:
  0.6 0.7 copy-start
  1.3 42.1 %copy-start.1 = (bf16[1,1,4096,32]{2,3,1,0:T(8,128)(2,1)S(1)}, bf16[1,1,4096,32]{2,3,1,0:T(8,128)(2,1)}, u32[]{:S(2)}) copy-start(bf16[1,1,4096,32]{2,3,1,0:T(8,128)(2,1)} %param.20) | copy-start | bytes 786436
  1.3 42.1 %copy-start.2 = (bf16[1,1,32,4096]{3,2,1,0:T(8,128)(2,1)S(1)}, bf16[1,1,32,4096]{3,2,1,0:T(8,128)(2,1)}, u32[]{:S(2)}) copy-start(bf16[1,1,32,4096]{3,2,1,0:T(8,128)(2,1)} %param.21) | copy-start | bytes 786436
  1.3 42.1 %copy-start.3 = (bf16[1,128,256]{2,1,0:T(8,128)(2,1)S(1)}, bf16[1,128,256]{2,1,0:T(8,128)(2,1)}, u32[]{:S(2)}) copy-start(bf16[1,128,256]{2,1,0:T(8,128)(2,1)} %param.17) | copy-start | bytes 196612
  1.3 42.2 %copy-start.4 = (bf16[1,128,256]{2,1,0:T(8,128)(2,1)S(1)}, bf16[1,128,256]{2,1,0:T(8,128)(2,1)}, u32[]{:S(2)}) copy-start(bf16[1,128,256]{2,1,0:T(8,128)(2,1)} %param.18) | copy-start | bytes 196612
  42.8 0.7 copy-start.5
  107.0 1.0 copy-start.6
  107.0 1.0 copy-start.7
  107.0 1.1 %copy-start.8 = (bf16[1,1,32,4096]{3,2,1,0:T(8,128)(2,1)}, bf16[1,1,32,4096]{3,2,1,0:T(8,128)(2,1)S(1)}, u32[]{:S(2)}) copy-start(bf16[1,1,32,4096]{3,2,1,0:T(8,128)(2,1)S(1)} %get-tuple-element.620) | copy-start | bytes 786436

commit v6 on v5

--- a/solution.py
+++ b/solution.py
@@ -32,6 +32,13 @@
     return row > col, row < col
 
 
+OFFSETS = [4 * dx + dy for dy in (2, 1, 3, 0) for dx in range(NX) if dx or dy]
+
+
+def partner(me, j):
+    return (me // NY + j // NY) % NX * NY + (me % NY + j % NY) % NY
+
+
 def remote(src, dst, send, recv, section, peer):
     return pltpu.make_async_remote_copy(
         src_ref=src, dst_ref=dst, send_sem=send, recv_sem=recv, device_id=(section, peer), device_id_type=MESH
@@ -53,8 +60,8 @@
     for load in loads:
         load.start()
     barrier = pltpu.get_barrier_semaphore()
-    for j in range(1, SECTIONS):
-        pl.semaphore_signal(barrier, inc=1, device_id=((me + j) % SECTIONS, peer), device_id_type=MESH)
+    for j in OFFSETS:
+        pl.semaphore_signal(barrier, inc=1, device_id=(partner(me, j), peer), device_id_type=MESH)
     for load in loads:
         load.wait()
     case_ref[0] = sum(
@@ -72,8 +79,8 @@
 
     def scatter(src, dst, send, recv):
         copies = []
-        for j in range(1, SECTIONS):
-            to = (me + j) % SECTIONS
+        for j in OFFSETS:
+            to = partner(me, j)
             cols = pl.ds(pl.multiple_of(to * SLICE, SLICE), SLICE)
             copies.append(remote(src.at[:, cols], dst.at[mine], send.at[j], recv.at[j], to, peer))
         for copy in copies:
@@ -367,14 +374,14 @@
         pl.semaphore_wait(barrier, SECTIONS - 1 + foreign + len(partners))
 
         def gradient_copy(src, dst, send, recv, j):
-            to = (me + j) % SECTIONS
+            to = partner(me, j)
             rows = pl.ds(pl.multiple_of(to * RANK, RANK), RANK)
             return remote(
                 src.at[rows], dst.at[foreign, :, place], send.at[j], recv.at[slot], to, peer - core + keeper
             )
 
         def scatter(src, dst, send, recv):
-            for j in range(1, SECTIONS):
+            for j in OFFSETS:
                 gradient_copy(src, dst, send, recv, j).start()
 
             @pl.when(foreign == 1)
@@ -386,7 +393,7 @@
                 dst[0, :, place] = src[pl.ds(pl.multiple_of(me * RANK, RANK), RANK), :]
 
         def scattered(src, dst, send, recv):
-            for j in range(1, SECTIONS):
+            for j in OFFSETS:
                 gradient_copy(src, dst, send, recv, j).wait_send()
 
             @pl.when(foreign == 1)
@@ -540,7 +547,7 @@
         adam_pairs(gup, gu, ru, 1, False)
         for chunk in second if zbits else first + second:
             next(chunk)
-        chunks = first + second
+        chunks = second + first if group > 2 and turn < half_width else first + second[::-1]
         while chunks:
             chunks = [chunk for chunk in chunks if next(chunk, "end") != "end"]
         for copy in pending:

time: 108 us -> 107 us (level)
  the two profiles are of different devices: /device:TPU:31 before, /device:TPU:25 now
where the time goes in v6:
time: 107 us; the launch traced here: 106 us
  Pallas kernels  102 us (95%)
  local copies, waits for them, and re-layouts  1.92 us (2%)
  between operations  1.42 us (1%)
    pallas_call x1, Pallas kernels, update(): pl.pallas_call(kernel, out_shape=(jax.ShapeDtypeStruct((rows_each, WIDTH)...  58 us
    pallas_call x1, Pallas kernels, products(): pl.pallas_call(products_kernel, out_shape=(jax.ShapeDtypeStruct((1,), jnp...  44.4 us

profile of v6, /device:TPU:25, one launch (start us, length us, event | category | flops | bytes accessed | tf_op | source)
XLA Modules:
  0.0 106.3 jit_solution(16286110775296734666)
XLA Ops:
  0.6 0.0 copy-start
  0.6 0.6 copy-done
  1.3 0.0 copy-start.1
  1.3 0.0 copy-start.2
  1.3 0.0 copy-start.3
  1.3 0.0 copy-start.4
  1.3 44.4 %products.1 = (s32[1]{0:T(128)}, bf16[512,896]{1,0:T(8,128)(2,1)S(1)}, bf16[512,256]{1,0:T(8,128)(2,1)S(1)}, bf16[512,256]{1,0:T(8,128)(2,1)S(1)}, bf16[512,512]...) custom-call(s32[4]{0:T(128)S(1)} %copy-done, ...), custom_call_target="tpu_custom_call" | custom-call | tf_op jit(solution)/shard_map/products/pallas_call | solution.py:215
  45.7 0.0 copy-start.5
  46.3 0.0 copy-done.1
  46.3 0.0 copy-done.2
  46.3 0.0 copy-done.3
  46.3 0.0 copy-done.4
  46.4 0.1 copy-done.5
  46.4 58.6 %conditional.1 = (bf16[96,4096]{1,0:T(8,128)(2,1)S(1)}, bf16[1,1,32,4096]{3,2,1,0:T(8,128)(2,1)S(1)}, bf16[1,1,32,4096]{3,2,1,0:T(8,128)(2,1)S(1)}, bf16[1,1,32,4096]{3,2,1,0:T(8,128)(2,1)S(1)}) conditional(s32[]{:T(128)} %bitcast.5, (bf16[512,896]{1,0:T(8,128)(2,1)S(1)}, bf16[512,256]{1,0:T(8,128)(2,1)S(1)}, ...), branch_computations={%region_0.0_spmd.clone.clone, %region_1.0_spmd.clone.clone, %regio... | conditional | bytes 1572896 | solution.py:610
  46.4 58.0 %update_2.3 = (bf16[96,4096]{1,0:T(8,128)(2,1)S(1)}, bf16[96,4096]{1,0:T(8,128)(2,1)S(1)}) custom-call(bf16[512,896]{1,0:T(8,128)(2,1)S(1)} %get-tuple-element.667.x_ref, bf16[512,256]{1,0:T(8,128)(2,1)S(1)} %get-tuple-element.668.af_ref, bf16[512,256]{1,0:T(8,128)(2,1)S(1)} %get-tuple-element.669.bf_ref, bf16[512,512]{1,0:T(8,128)(2,1)S(1)} %get-tuple-element.670.xt, ...), custom_call_target="tpu_custom_call" | custom-call | tf_op jit(solution)/shard_map/cond/branch_2_fun/update_2/pallas_call | solution.py:583
  104.5 0.1 slice_bitcast_fusion.6
  105.1 0.0 copy-start.6
  105.1 0.0 copy-start.7
  105.1 0.0 copy-start.8
  105.1 1.0 slice_bitcast_fusion.21
  106.1 0.0 copy-done.6
  106.1 0.0 copy-done.7
  106.1 0.1 copy-done.8
Async XLA Ops:
  0.6 0.7 copy-start
  1.3 45.0 %copy-start.1 = (bf16[1,1,4096,32]{2,3,1,0:T(8,128)(2,1)S(1)}, bf16[1,1,4096,32]{2,3,1,0:T(8,128)(2,1)}, u32[]{:S(2)}) copy-start(bf16[1,1,4096,32]{2,3,1,0:T(8,128)(2,1)} %param.20) | copy-start | bytes 786436
  1.3 45.0 %copy-start.2 = (bf16[1,1,32,4096]{3,2,1,0:T(8,128)(2,1)S(1)}, bf16[1,1,32,4096]{3,2,1,0:T(8,128)(2,1)}, u32[]{:S(2)}) copy-start(bf16[1,1,32,4096]{3,2,1,0:T(8,128)(2,1)} %param.21) | copy-start | bytes 786436
  1.3 45.0 %copy-start.3 = (bf16[1,128,256]{2,1,0:T(8,128)(2,1)S(1)}, bf16[1,128,256]{2,1,0:T(8,128)(2,1)}, u32[]{:S(2)}) copy-start(bf16[1,128,256]{2,1,0:T(8,128)(2,1)} %param.17) | copy-start | bytes 196612
  1.3 45.0 %copy-start.4 = (bf16[1,128,256]{2,1,0:T(8,128)(2,1)S(1)}, bf16[1,128,256]{2,1,0:T(8,128)(2,1)}, u32[]{:S(2)}) copy-start(bf16[1,128,256]{2,1,0:T(8,128)(2,1)} %param.18) | copy-start | bytes 196612
  45.7 0.7 copy-start.5
  105.1 1.0 copy-start.6
  105.1 1.0 copy-start.7
  105.1 1.1 %copy-start.8 = (bf16[1,1,32,4096]{3,2,1,0:T(8,128)(2,1)}, bf16[1,1,32,4096]{3,2,1,0:T(8,128)(2,1)S(1)}, u32[]{:S(2)}) copy-start(bf16[1,1,32,4096]{3,2,1,0:T(8,128)(2,1)S(1)} %get-tuple-element.620) | copy-start | bytes 786436
